TPU v7x, 32 devices: a whole 2x2x4 slice. The times are simulated.
32 devices in a mesh: groups: 2 (over x), replica: 4 (over y, core), tensor: 4 (over z).
Axes of the slice: x: 2, y: 2, z: 4, core: 2. Of those that a mesh axis runs over, the one named last changes fastest.
Arguments:
- tokens: bfloat16 [128, 5120], P('groups', 'replica'), parts along dimension 0, may hold values from -6 to 6
- gate_matrix: bfloat16 [5120, 25600], P('replica', 'tensor'), may hold values from -0.078125 to 0.078125
- up_matrix: bfloat16 [5120, 25600], P('replica', 'tensor'), may hold values from -0.078125 to 0.078125
- down_weight: bfloat16 [25600, 5120], P('tensor', 'replica'), may hold values from -0.0390625 to 0.0390625
- adapter_down: bfloat16 [32, 2, 16, 5120], P('replica'), may hold values from -0.078125 to 0.078125
- adapter_up: bfloat16 [32, 2, 16, 25600], P('replica', None, None, 'tensor'), may hold values from -1.5 to 1.5
- adapter_ids: int32 [128], P('groups'), parts along dimension 0, may hold values from 0 to 31, as said below
- adapter_slot: int32 [64], P('groups'), parts along dimension 0, may hold values from 0 to 31, as said below
Outputs:
- layer_output: bfloat16 [128, 5120], P('groups', 'replica'), parts along dimension 0
There are 2 independent parts, one for each index of `groups`. A program takes and returns all parts, laid end to end along the dimension named above; an argument that names none is the same for every part. Nothing has to cross between parts.
Inputs may be any that keep to these rules, and one draw needn't show every extreme that they name: `adapter_ids`: adapter a is stored in slot adapter_slot[a]; slots s * 8 to (s + 1) * 8 - 1 are those of index s of replica. In each aligned block of 16 rows, at most 8 rows use adapters stored on one index of replica, and in every block some index gets exactly 8. `adapter_slot`: A permutation of the adapters' slots.
All inputs are finite; a program needn't handle non-finite values.
Results may differ from a plain program's by a relative error of at most 0.0056.
Values may be sent and summed in bfloat16 or wider, within the bound.
No kernel may reach another device: no remote copies, remote signals or barrier semaphores. Data moves between devices by JAX's collectives and lax.ppermute only.
A program may use at most 128 MiB of HBM per device.

v0:
```python
import jax
import jax.numpy as jnp
from jax import lax
from jax.sharding import PartitionSpec as P

low_rank_scale = 0.5


def row_routes(adapter_ids, adapter_slot, stored, blocks, block_rows, capacity):
    row_count = adapter_ids.shape[0]
    table_size = adapter_slot.shape[0]
    matched = adapter_ids[:, None] == jnp.arange(table_size, dtype=jnp.int32)[None, :]
    row_slot_lookup = jnp.sum(jnp.where(matched, adapter_slot[None, :], 0), axis=1)
    owners = row_slot_lookup // stored
    local_index = row_slot_lookup % stored
    grouped = owners.reshape(blocks, block_rows)
    within = jnp.arange(block_rows, dtype=jnp.int32)
    alike = grouped[:, :, None] == grouped[:, None, :]
    before = within[:, None] > within[None, :]
    places = jnp.sum(jnp.logical_and(alike, before[None]), axis=2).reshape(row_count)
    column = jnp.arange(row_count, dtype=jnp.int32) // block_rows * capacity + places
    target = owners * (blocks * capacity) + column
    slot_count = blocks * blocks * capacity
    source_row = (
        jnp.zeros((slot_count,), jnp.int32).at[target].set(jnp.arange(row_count, dtype=jnp.int32))
    )
    filled = jnp.zeros((slot_count,), jnp.int32).at[target].set(1)
    tagged = jnp.full((slot_count,), -1, jnp.int32).at[target].set(local_index)
    return (source_row, filled, tagged)


def shards(
    tokens, gate_matrix, up_matrix, down_weight, adapter_down, adapter_up, adapter_ids, adapter_slot
):
    replicas = lax.axis_size("replica")
    my_index = lax.axis_index("replica")
    row_count = tokens.shape[0]
    block_rows = row_count // replicas
    capacity = 2 * block_rows // replicas
    stored = adapter_down.shape[0]
    rank_width = adapter_down.shape[2]
    full_width = adapter_down.shape[3]
    local_cols = tokens.shape[1]
    resident_units = gate_matrix.shape[1]
    slot_holders = replicas * capacity
    source_row, filled, tagged = row_routes(
        adapter_ids, adapter_slot, stored, replicas, block_rows, capacity
    )
    outgoing = jnp.take(tokens, source_row, axis=0) * filled[:, None].astype(jnp.bfloat16)
    outgoing = outgoing.reshape(replicas, slot_holders, local_cols)
    labels = tagged.reshape(replicas, slot_holders, 1)
    arrived = lax.all_to_all(outgoing, "replica", split_axis=0, concat_axis=2, tiled=True)
    marks = lax.all_to_all(labels, "replica", split_axis=0, concat_axis=2, tiled=True)
    slot_rows = arrived.reshape(-1, full_width)
    item_count = slot_rows.shape[0]
    first_label = marks.reshape(item_count, -1)[:, 0]
    chosen = first_label[:, None] == jnp.arange(stored, dtype=jnp.int32)[None, :]
    flat_down = adapter_down.reshape(stored * 2 * rank_width, full_width)
    every = lax.dot_general(
        slot_rows, flat_down, (((1,), (1,)), ((), ())), preferred_element_type=jnp.float32
    )
    every = every.reshape(item_count, stored, 2 * rank_width)
    shrink = jnp.sum(jnp.where(chosen[:, :, None], every, 0.0), axis=1).astype(jnp.bfloat16)
    dispersed = jnp.where(chosen[:, :, None], shrink[:, None, :], jnp.zeros((), jnp.bfloat16))
    dispersed = dispersed.reshape(item_count, stored, 2, rank_width)
    gate_portion = jnp.dot(
        dispersed[:, :, 0, :].reshape(item_count, stored * rank_width),
        adapter_up[:, 0].reshape(stored * rank_width, -1),
        preferred_element_type=jnp.float32,
    )
    up_portion = jnp.dot(
        dispersed[:, :, 1, :].reshape(item_count, stored * rank_width),
        adapter_up[:, 1].reshape(stored * rank_width, -1),
        preferred_element_type=jnp.float32,
    )
    low_rank_delta = (low_rank_scale * jnp.stack([gate_portion, up_portion], axis=1)).astype(
        jnp.bfloat16
    )
    incoming_delta = low_rank_delta[None]
    gathered_back = lax.all_to_all(
        incoming_delta.reshape(replicas, capacity, 2, resident_units),
        "replica",
        split_axis=0,
        concat_axis=0,
        tiled=True,
    )
    low_rank_delta = gathered_back.reshape(slot_holders, 2, resident_units)
    positions = lax.dynamic_slice_in_dim(
        source_row.reshape(replicas, replicas, capacity), my_index, 1, 1
    ).reshape(slot_holders)
    delta_full = (
        jnp.zeros((row_count, 2, resident_units), jnp.float32)
        .at[positions]
        .add(low_rank_delta.astype(jnp.float32))
    )
    gate_portion = jnp.dot(tokens, gate_matrix, preferred_element_type=jnp.float32)
    up_portion = jnp.dot(tokens, up_matrix, preferred_element_type=jnp.float32)
    summed_rows = lax.psum_scatter(
        jnp.stack([gate_portion, up_portion], axis=1) + delta_full,
        "replica",
        scatter_dimension=0,
        tiled=True,
    )
    hidden = (jax.nn.silu(summed_rows[:, 0]) * summed_rows[:, 1]).astype(jnp.bfloat16)
    projected = jnp.dot(
        lax.all_gather(hidden, "replica", axis=0, tiled=True),
        down_weight,
        preferred_element_type=jnp.float32,
    )
    summed = lax.psum(projected, "tensor")
    return summed.astype(jnp.bfloat16)


def solution(mesh):
    placed = (
        P("groups", "replica"),
        P("replica", "tensor"),
        P("replica", "tensor"),
        P("tensor", "replica"),
        P("replica", None, None, None),
        P("replica", None, None, "tensor"),
        P("groups"),
        P("groups"),
    )
    return jax.shard_map(
        shards, mesh=mesh, in_specs=placed, out_specs=P("groups", "replica"), check_vma=False
    )
```

profile of v0, /device:TPU:0, one launch (start us, length us, event | category | flops | bytes accessed | tf_op | source)
XLA Modules:
  0.0 202.4 jit_solution(2382094654560312156)
XLA Ops:
  6.5 0.9 select_reduce_fusion
  7.9 0.8 scatter_custom_fusion.1
  9.3 4.2 %all-to-all-start = ((s32[4,32,1]{1,2,0:T(1,128)}), s32[4,32,1]{1,2,0:T(1,128)S(1)}, u32[]{:S(2)}, u32[]{:S(2)}) async-start(s32[4,32,1]{1,2,0:T(1,128)} %bitcast.5), calls=%async_computation | async-start | bytes 4096 | tf_op jit(solution)/shard_map/all_to_all | solution.py:53
  15.4 2.1 %gather_fusion = bf16[128,1280]{1,0:T(8,128)(2,1)S(1)} fusion(bf16[64,1280]{1,0:T(8,128)(2,1)} %param.8, s32[1024]{0:T(1024)S(1)} %pad_clamp_fusion), kind=kCustom, calls=%fused_computation | custom fusion | bytes 655872 | tf_op jit(solution)/shard_map/jit(_take)/gather | solution.py:49
  17.5 10.0 %convolution_bitcast_fusion = f32[64,1,6400]{2,0,1:T(8,128)} fusion(bf16[64,1280]{1,0:T(8,128)(2,1)} %param.8, bf16[1280,6400]{1,0:T(8,128)(2,1)} %param.10), kind=kOutput, calls=%fused_computation.5 | convolution fusion | flops 1048576000 | bytes 18186240 | tf_op jit(solution)/shard_map/dot_general | solution.py:97
  27.5 1.0 copy-done.3
  28.5 4.2 %convolution_bitcast_fusion.1 = f32[64,1,6400]{2,0,1:T(8,128)} fusion(bf16[64,1280]{1,0:T(8,128)(2,1)S(1)} %copy-done.2, bf16[1280,6400]{1,0:T(8,128)(2,1)S(1)} %copy-done.3), kind=kOutput, calls=%fused_computation.6 | convolution fusion | flops 1048576000 | bytes 18186240 | tf_op jit(solution)/shard_map/dot_general | solution.py:96
  32.7 0.8 select_multiply_fusion
  33.5 3.5 %all-to-all-start.1 = ((bf16[4,32,1280]{2,1,0:T(8,128)(2,1)}), bf16[4,32,1280]{2,1,0:T(8,128)(2,1)S(1)}, u32[]{:S(2)}, u32[]{:S(2)}) async-start(bf16[4,32,1280]{2,1,0:T(8,128)(2,1)} %select_multiply_fusion), calls=%async_computation.1 | async-start | bytes 655360 | tf_op jit(solution)/shard_map/all_to_all | solution.py:52
  37.1 6.6 %all-to-all-done.1 = bf16[4,32,1280]{2,1,0:T(8,128)(2,1)S(1)} async-done(((bf16[4,32,1280]{2,1,0:T(8,128)(2,1)}), bf16[4,32,1280]{2,1,0:T(8,128)(2,1)S(1)}, u32[]{:S(2)}, u32[]{:S(2)}) %all-to-all-start.1) | async-done | bytes 327712 | tf_op jit(solution)/shard_map/all_to_all | solution.py:52
  44.2 2.2 %fusion.5 = bf16[32,32]{1,0:T(8,128)(2,1)S(1)} fusion(bf16[32,5120,1]{1,0,2:T(8,128)(2,1)S(1)} %reshape.359, bf16[8,32,5120]{2,1,0:T(8,128)(2,1)S(1)} %bitcast.82, pred[32,8]{0,1:T(8,128)(4,1)S(1)} %iota_compare_fusion.2), kind=kOutput, calls=%fused_computation.17 | convolution fusion | flops 83901440 | bytes 2951424 | tf_op jit(solution)/shard_map/dot_general | solution.py:59
  46.7 2.2 %convolution_bitcast_fusion.2 = f32[4,8,1,6400]{3,1,0,2:T(8,128)S(1)} fusion(bf16[8,2,16,6400]{3,2,1,0:T(8,128)(2,1)} %param.13, bf16[4,8,8,16]{3,2,1,0:T(8,128)(2,1)S(1)} %bitcast.86), kind=kOutput, calls=%fused_computation.7 | convolution fusion | flops 52428800 | bytes 2465792 | tf_op jit(solution)/shard_map/dot_general | solution.py:71
  49.7 1.0 copy.62
  50.7 3.5 %all-to-all-start.2 = ((bf16[4,8,2,6400]{3,1,2,0:T(8,128)(2,1)}), bf16[4,8,2,6400]{3,1,2,0:T(8,128)(2,1)S(1)}, u32[]{:S(2)}, u32[]{:S(2)}) async-start(bf16[4,8,2,6400]{3,1,2,0:T(8,128)(2,1)} %copy.62), calls=%async_computation.2 | async-start | bytes 1638400 | tf_op jit(solution)/shard_map/all_to_all | solution.py:80
  54.5 3.4 %pad_maximum_fusion = f32[64,2,6400]{2,0,1:T(8,128)} fusion(f32[64,1,6400]{2,0,1:T(8,128)S(1)} %copy-done.4, f32[64,1,6400]{2,0,1:T(8,128)} %convolution_bitcast_fusion.1), kind=kLoop, calls=%fused_computation.9 | loop fusion | flops 819200 | bytes 6553600 | tf_op jit(solution)/shard_map/stack | solution.py:99
  58.0 6.1 %copy.64 = f32[64,2,6400]{2,1,0:T(2,128)} copy(f32[64,2,6400]{2,0,1:T(8,128)} %pad_maximum_fusion) | data formatting | bytes 6553600 | tf_op jit(solution)/shard_map/stack | solution.py:99
  64.2 2.0 all-to-all-done.2
  66.3 1.3 copy.65
  67.6 10.8 %scatter_fusion = f32[64,2,6400]{2,1,0:T(2,128)} fusion(f32[64,2,6400]{2,1,0:T(2,128)} %copy.64, s32[32]{0:T(128)S(1)} %fusion.16, f32[32,2,6400]{2,1,0:T(2,128)S(1)} %copy.65), kind=kCustom, calls=%fused_computation.4 | custom fusion | flops 409600 | bytes 4915328 | tf_op jit(solution)/shard_map/scatter-add | solution.py:94
  79.7 70.2 %all-reduce.4.cloned.1.call-done = f32[64,2,6400]{2,1,0:T(2,128)} async-done(((f32[64,2,6400]{2,1,0:T(2,128)}), f32[64,2,6400]{2,1,0:T(2,128)}) %all-reduce.4.cloned.1.call-update) | async-done | bytes 3276816
  149.9 2.1 %constant_dynamic-slice_fusion = (f32[16,1,6400]{2,1,0:T(1,128)S(1)}, f32[16,1,6400]{2,1,0:T(1,128)S(1)}) fusion(f32[64,2,6400]{2,1,0:T(2,128)} %all-reduce.4.cloned.1.call-done, u32[]{:T(128)S(6)} %multiply.1, u32[]{:T(128)S(6)} %convert.3), kind=kLoop, calls=%fused_computation.61 | loop fusion | bytes 1638408 | tf_op jit(solution)/shard_map/slice | solution.py:104
  152.1 8.3 %all_gather.3 = bf16[64,6400]{1,0:T(8,128)(2,1)S(1)} all-gather(bf16[16,6400]{1,0:T(8,128)(2,1)S(1)} %fusion.6), channel_id=1, replica_groups=mesh['groups'=2,'replica'=4,'tensor'=4] {'replica'}, dimensions={0}, use_global_device_ids=true | all-gather | bytes 1024000 | tf_op jit(solution)/shard_map/all_gather | solution.py:106
  160.4 8.8 %fusion.24 = f32[64,1280]{1,0:T(8,128)S(1)} fusion(bf16[64,6400]{1,0:T(8,128)(2,1)S(1)} %all_gather.3, bf16[6400,1280]{1,0:T(8,128)(2,1)} %param.11), kind=kOutput, calls=%fused_computation.72 | convolution fusion | flops 1048576000 | bytes 17530880 | tf_op jit(solution)/shard_map/dot_general | solution.py:105
  169.2 26.3 %all-reduce.5 = bf16[64,1280]{1,0:T(8,128)(2,1)} all-reduce(f32[64,1280]{1,0:T(8,128)S(1)} %fusion.24), channel_id=1, replica_groups=mesh['groups'=2,'replica'=4,'tensor'=4] {'tensor'}, use_global_device_ids=true, to_apply=%region_8.9 | all-reduce | flops 81920 | bytes 491520 | tf_op jit(solution)/shard_map/psum | solution.py:110
  (52 shorter events, 5.8 us)
Async XLA Ops:
  6.5 37.7 %copy-start = (bf16[8,2,16,5120]{3,2,1,0:T(8,128)(2,1)S(1)}, bf16[8,2,16,5120]{3,2,1,0:T(8,128)(2,1)}, u32[]{:S(2)}) copy-start(bf16[8,2,16,5120]{3,2,1,0:T(8,128)(2,1)} %param.12) | copy-start | bytes 7864324
  9.3 24.2 %all-to-all-start = ((s32[4,32,1]{1,2,0:T(1,128)}), s32[4,32,1]{1,2,0:T(1,128)S(1)}, u32[]{:S(2)}, u32[]{:S(2)}) async-start(s32[4,32,1]{1,2,0:T(1,128)} %bitcast.5), calls=%async_computation | async-start | bytes 4096 | tf_op jit(solution)/shard_map/all_to_all | solution.py:53
  17.4 10.1 %copy-start.2 = (bf16[64,1280]{1,0:T(8,128)(2,1)S(1)}, bf16[64,1280]{1,0:T(8,128)(2,1)}, u32[]{:S(2)}) copy-start(bf16[64,1280]{1,0:T(8,128)(2,1)} %param.8) | copy-start | bytes 491524
  17.5 11.1 %copy-start.3 = (bf16[1280,6400]{1,0:T(8,128)(2,1)S(1)}, bf16[1280,6400]{1,0:T(8,128)(2,1)}, u32[]{:S(2)}) copy-start(bf16[1280,6400]{1,0:T(8,128)(2,1)} %param.9) | copy-start | bytes 49152004
  33.5 10.2 %all-to-all-start.1 = ((bf16[4,32,1280]{2,1,0:T(8,128)(2,1)}), bf16[4,32,1280]{2,1,0:T(8,128)(2,1)S(1)}, u32[]{:S(2)}, u32[]{:S(2)}) async-start(bf16[4,32,1280]{2,1,0:T(8,128)(2,1)} %select_multiply_fusion), calls=%async_computation.1 | async-start | bytes 655360 | tf_op jit(solution)/shard_map/all_to_all | solution.py:52
  46.6 2.4 %copy-start.5 = (bf16[8,2,16,6400]{3,2,1,0:T(8,128)(2,1)S(1)}, bf16[8,2,16,6400]{3,2,1,0:T(8,128)(2,1)}, u32[]{:S(2)}) copy-start(bf16[8,2,16,6400]{3,2,1,0:T(8,128)(2,1)} %param.13) | copy-start | bytes 9830404
  49.6 4.8 %copy-start.4 = (f32[64,1,6400]{2,0,1:T(8,128)S(1)}, f32[64,1,6400]{2,0,1:T(8,128)}, u32[]{:S(2)}) copy-start(f32[64,1,6400]{2,0,1:T(8,128)} %convolution_bitcast_fusion) | copy-start | bytes 4915204
  50.7 15.5 %all-to-all-start.2 = ((bf16[4,8,2,6400]{3,1,2,0:T(8,128)(2,1)}), bf16[4,8,2,6400]{3,1,2,0:T(8,128)(2,1)S(1)}, u32[]{:S(2)}, u32[]{:S(2)}) async-start(bf16[4,8,2,6400]{3,1,2,0:T(8,128)(2,1)} %copy.62), calls=%async_computation.2 | async-start | bytes 1638400 | tf_op jit(solution)/shard_map/all_to_all | solution.py:80
  54.2 95.7 %all-reduce.4.cloned.1.call-start = ((), (), s32[]{:S(2)}) async-start(), calls=%async_computation.3 | async-start | bytes 6553600
  67.6 10.9 %copy-start.6 = (u32[32]{0:T(128)S(1)}, u32[32]{0:T(128)}, u32[]{:S(2)}) copy-start(u32[32]{0:T(128)} %constant.86) | copy-start | bytes 388
  160.4 35.1 %copy-start.1 = (bf16[8,2,16,5120]{3,2,1,0:T(8,128)(2,1)S(1)}, bf16[8,2,16,5120]{3,2,1,0:T(8,128)(2,1)}, u32[]{:S(2)}) copy-start(bf16[8,2,16,5120]{3,2,1,0:T(8,128)(2,1)} %param.12) | copy-start | bytes 7864324
Sparse Core Ops, SparseCore 0:
  78.5 71.3 all-reduce.3
where the time goes:
time: 203 us; the launch traced here: 202 us
  waiting for transfers between devices  78.9 us (39%)
  blocking collectives  34.6 us (17%)
  matrix products  27.9 us (14%)
  local copies, waits for them, and re-layouts  18.6 us (9%)
  other arithmetic  16.6 us (8%)
  between operations  14.3 us (7%)
  starting transfers between devices  11.4 us (6%)
    unnamed x2, waiting for transfers between devices  70.3 us
    psum x1, blocking collectives, shards(): summed = lax.psum(projected, 'tensor')  26.3 us
    scatter-add x1, other arithmetic, shards(): delta_full = jnp.zeros((row_count, 2, resident_units), jnp.float32).at[po...  10.8 us
    dot_general x1, matrix products, shards(): up_portion = jnp.dot(tokens, up_matrix, preferred_element_type=jnp.float32)  10 us
    dot_general x1, matrix products, shards(): jnp.dot(lax.all_gather(hidden, 'replica', axis=0, tiled=True), down_weigh...  8.77 us
    all_gather x1, blocking collectives, shards(): lax.all_gather(hidden, 'replica', axis=0, tiled=True)  8.29 us
    all_to_all x1, waiting for transfers between devices, shards(): lax.all_to_all(outgoing, 'replica', split_axis=0, concat_axis=2, tiled=True)  6.59 us
    another operation x1, local copies, waits for them, and re-layouts, shards(): jnp.stack([gate_portion, up_portion], axis=1) + delta_full  6.15 us
  transfers between devices with their start and end apart: 4, of which 3 were waited for; matrix products, arithmetic and copies ran while one was open for 14% of the time, Pallas kernels for 0%

commit v1 on v0

v1 whole, which is shorter than its diff:
```python
import jax
import jax.numpy as jnp
from jax import lax
from jax.experimental import pallas as pl
from jax.experimental.pallas import tpu as pltpu
from jax.sharding import PartitionSpec as P

low_rank_scale = 0.5
f32 = jnp.float32
bf16 = jnp.bfloat16
MIB = 1 << 20
CHUNKS = (1280, 1280, 1280, 1280, 1280)
GATHERED = False


def dot(a, b):
    return jnp.dot(a, b, preferred_element_type=f32)


def core_swap(value, replicas):
    return lax.ppermute(value, "replica", [(i, i ^ 1) for i in range(replicas)])


def from_chip(value, replicas, step, flip=0):
    pairs = [((i + 2 * step) % replicas ^ flip, i) for i in range(replicas)]
    return lax.ppermute(value, "replica", pairs)


def shrink_kernel(source_ref, ids_ref, slots_ref, order_ref, down_ref, *refs):
    pieces, spread_ref = refs[:-1], refs[-1]
    rows, width = pieces[0].shape
    stored, _, rank, full = down_ref.shape
    table = stored * 2 * rank
    total = jnp.zeros((rows, table), f32)
    for j, piece in enumerate(pieces):
        columns = pl.ds(pl.multiple_of(source_ref[j] * width, 128), width)
        part = down_ref[:, :, :, columns].reshape(table, width)
        total += lax.dot_general(piece[...], part, (((1,), (1,)), ((), ())), preferred_element_type=f32)
    shrink = total.astype(bf16).astype(f32)
    ids = ids_ref[...]
    known = lax.broadcasted_iota(jnp.int32, (rows, slots_ref.shape[1]), 1)
    slot = jnp.sum(jnp.where(ids == known, slots_ref[...], 0), axis=1, keepdims=True)
    local = slot - source_ref[len(pieces)] * stored
    column = lax.broadcasted_iota(jnp.int32, (rows, table), 1)
    for p in range(2):
        first = local * (2 * rank) + p * rank
        mine = jnp.logical_and(column >= first, column < first + rank)
        picked = jnp.where(mine, shrink, 0.0).astype(bf16)
        spread_ref[p] = dot(order_ref[...], picked).astype(bf16)


def shrink_rows(pieces, sources, ids, slots, order, adapter_down):
    rows = ids.shape[0]
    stored, _, rank, _ = adapter_down.shape
    vmem = pl.BlockSpec(memory_space=pltpu.VMEM)
    return pl.pallas_call(
        shrink_kernel,
        out_shape=jax.ShapeDtypeStruct((2, rows, stored * 2 * rank), bf16),
        in_specs=[pl.BlockSpec(memory_space=pltpu.SMEM)] + [vmem] * (4 + len(pieces)),
        out_specs=vmem,
        compiler_params=pltpu.CompilerParams(vmem_limit_bytes=24 * MIB),
        cost_estimate=pl.CostEstimate(
            flops=2 * adapter_down.size * rows, bytes_accessed=2 * adapter_down.size, transcendentals=0
        ),
        name="shrink",
    )(sources, ids.reshape(rows, 1), slots.reshape(1, -1), order, adapter_down, *pieces)


def shards(
    tokens, gate_matrix, up_matrix, down_weight, adapter_down, adapter_up, adapter_ids, adapter_slot
):
    replicas, depth = lax.axis_size("replica"), lax.axis_size("tensor")
    chips = replicas // 2
    me, layer = lax.axis_index("replica"), lax.axis_index("tensor")
    rows = tokens.shape[0]
    block = rows // replicas
    half = rows // 2
    units = gate_matrix.shape[1]
    place = jnp.arange(rows, dtype=jnp.int32)
    nth, within = place // block, place % block
    chip = (me // 2 + nth % chips) % chips
    natural = (chip * 2 + ((me % 2) ^ (nth // chips))) * block + within
    order = (natural[:, None] == place[None, :]).astype(bf16)

    pieces = [tokens, core_swap(tokens, replicas)]
    sources = [me, me ^ 1]
    for step in range(1, chips):
        for flip in range(2):
            pieces.append(from_chip(tokens, replicas, step, flip))
            sources.append((me + 2 * step) % replicas ^ flip)
    mixed = dot(order, tokens).astype(bf16)
    spread = shrink_rows(
        pieces, jnp.stack(sources + [me]).astype(jnp.int32), adapter_ids, adapter_slot, order, adapter_down
    )
    expand = adapter_up.reshape(-1, units)

    widths = CHUNKS if sum(CHUNKS) == units else (units,)
    total = None
    start = 0
    for width in widths:
        cut = slice(start, start + width)
        start += width
        sums = []
        for p, matrix in enumerate((gate_matrix, up_matrix)):
            delta = (low_rank_scale * dot(spread[p], expand[:, cut])).astype(bf16)
            sums.append(dot(mixed, matrix[:, cut]) + delta.astype(f32))
        both = jnp.stack(sums)
        own = both[:, :half] + core_swap(both[:, half:].astype(bf16), replicas).astype(f32)
        if GATHERED:
            away = own.astype(bf16)
            own = own[:, :block]
            for step in range(1, chips):
                own = own + from_chip(
                    away[:, step * block : (step + 1) * block], replicas, chips - step
                ).astype(f32)
        else:
            away = own.astype(bf16)
            for step in range(1, chips):
                got = from_chip(away, replicas, step).astype(f32)
                got = jnp.roll(got, step * block, axis=1) if chips > 2 else jnp.concatenate(
                    [got[:, block:], got[:, :block]], axis=1
                )
                own = own + got
        hidden = (jax.nn.silu(own[0]) * own[1]).astype(bf16)
        if GATHERED:
            hidden = jnp.concatenate(
                [hidden] + [from_chip(hidden, replicas, step) for step in range(1, chips)], axis=0
            )
        hidden = jnp.concatenate([hidden, core_swap(hidden, replicas)], axis=0)
        part = dot(hidden, down_weight[cut])
        total = part if total is None else total + part

    share = rows // depth
    blocks = total.reshape(depth, share, -1)
    pick = [lax.dynamic_index_in_dim(blocks, (layer + s) % depth, 0, False) for s in range(depth)]
    mine = pick[0]
    for s in range(1, depth):
        pairs = [(i, (i + s) % depth) for i in range(depth)]
        mine = mine + lax.ppermute(pick[s].astype(bf16), "tensor", pairs).astype(f32)
    mine = mine.astype(bf16)
    got = [mine]
    for s in range(1, depth):
        pairs = [((i + s) % depth, i) for i in range(depth)]
        got.append(lax.ppermute(mine, "tensor", pairs))
    held = (layer + place // share) % depth * share + place % share
    gather = (held[:, None] == place[None, :]).astype(bf16)
    back = dot(order.T, gather.T).astype(bf16)
    return dot(back, jnp.concatenate(got, axis=0)).astype(bf16)


def solution(mesh):
    placed = (
        P("groups", "replica"),
        P("replica", "tensor"),
        P("replica", "tensor"),
        P("tensor", "replica"),
        P("replica", None, None, None),
        P("replica", None, None, "tensor"),
        P("groups"),
        P("groups"),
    )
    return jax.shard_map(
        shards, mesh=mesh, in_specs=placed, out_specs=P("groups", "replica"), check_vma=False
    )
```

time: 203 us -> 93.2 us (0.46)
  waiting for transfers between devices: 78.9 us -> 27.3 us
  blocking collectives: 34.6 us -> 0 us
  other arithmetic: 16.6 us -> 0.98 us
  local copies, waits for them, and re-layouts: 18.6 us -> 4.32 us
  between operations: 14.3 us -> 0.36 us
  matrix products: 27.9 us -> 37.3 us
  starting transfers between devices: 11.4 us -> 20.6 us
    unnamed x2 -> x0, waiting for transfers between devices: 70.3 us -> none
    ppermute x0 -> x24, waiting for transfers between devices: none -> 27.3 us  [the longest x7 19.5 us: from_chip(): return lax.ppermute(value, 'replica', pairs)]
    psum x1 -> x0, blocking collectives: 26.3 us -> none  [shards(): summed = lax.psum(projected, 'tensor')]
    ppermute x0 -> x24, starting transfers between devices: none -> 20.6 us  [the longest x7 8.59 us: from_chip(): return lax.ppermute(value, 'replica', pairs)]
    all_to_all x3 -> x0, starting transfers between devices: 11.2 us -> none  [the longest x1 4.24 us: shards(): lax.all_to_all(labels, 'replica', split_axis=0, concat_axis=2, tiled=True)]
    scatter-add x1 -> x0, other arithmetic: 10.8 us -> none  [shards(): delta_full = jnp.zeros((row_count, 2, resident_units), jnp.float32).at[po...]
    dot_general x6 -> x27, matrix products: 27.9 us -> 37.3 us  [dot(): return jnp.dot(a, b, preferred_element_type=f32)]
    all_to_all x3 -> x0, waiting for transfers between devices: 8.61 us -> none  [the longest x1 6.59 us: shards(): lax.all_to_all(outgoing, 'replica', split_axis=0, concat_axis=2, tiled=True)]
  transfers between devices with their start and end apart: 4 -> 24, of which waited for: 3 -> 13; matrix products, arithmetic and copies ran while one was open for 14% -> 21% of each run, Pallas kernels for 0% -> 0%
where the time goes in v1:
time: 93.2 us; the launch traced here: 92.5 us
  matrix products  37.3 us (40%)
  waiting for transfers between devices  27.3 us (29%)
  starting transfers between devices  20.6 us (22%)
  local copies, waits for them, and re-layouts  4.32 us (5%)
  Pallas kernels  1.61 us (2%)
  other arithmetic  0.98 us (1%)
    dot_general x27, matrix products, dot(): return jnp.dot(a, b, preferred_element_type=f32)  37.3 us
    ppermute x7, waiting for transfers between devices, from_chip(): return lax.ppermute(value, 'replica', pairs)  19.5 us
    ppermute x7, starting transfers between devices, from_chip(): return lax.ppermute(value, 'replica', pairs)  8.59 us
    ppermute x3, starting transfers between devices, shards(): lax.ppermute(pick[s].astype(bf16), 'tensor', pairs).astype(f32)  5.68 us
    ppermute x3, waiting for transfers between devices, shards(): got.append(lax.ppermute(mine, 'tensor', pairs))  5.15 us
    ppermute x3, starting transfers between devices, shards(): got.append(lax.ppermute(mine, 'tensor', pairs))  3.81 us
    unnamed x16, local copies, waits for them, and re-layouts  3.34 us
    ppermute x3, waiting for transfers between devices, shards(): lax.ppermute(pick[s].astype(bf16), 'tensor', pairs).astype(f32)  2.69 us
  transfers between devices with their start and end apart: 24, of which 13 were waited for; matrix products, arithmetic and copies ran while one was open for 21% of the time, Pallas kernels for 0%

profile of v1, /device:TPU:0, one launch (start us, length us, event | category | flops | bytes accessed | tf_op | source)
XLA Modules:
  0.0 92.5 jit_solution(7789884290819063294)
XLA Ops:
  0.5 2.5 %collective-permute-start.1 = (bf16[64,1280]{1,0:T(8,128)(2,1)}, bf16[64,1280]{1,0:T(8,128)(2,1)S(1)}, u32[]{:S(2)}, u32[]{:S(2)}) collective-permute-start(bf16[64,1280]{1,0:T(8,128)(2,1)} %refs_0_.1), channel_id=1, source_target_pairs={{8,0},{12,4},{0,8},{4,12},{9,1},{13,5},{1,9},{5,13},{10,2},{14,6},... | collective-permute-start | bytes 491528 | tf_op jit(solution)/shard_map/ppermute | solution.py:26
  5.2 3.0 %collective-permute-done.1.refs_2_ = bf16[64,1280]{1,0:T(8,128)(2,1)S(1)} collective-permute-done((bf16[64,1280]{1,0:T(8,128)(2,1)}, bf16[64,1280]{1,0:T(8,128)(2,1)S(1)}, u32[]{:S(2)}, u32[]{:S(2)}) %collective-permute-start.1) | collective-permute-done | bytes 163872 | tf_op jit(solution)/shard_map/ppermute | solution.py:26
  8.2 3.1 %collective-permute-done.2.refs_3_ = bf16[64,1280]{1,0:T(8,128)(2,1)S(1)} collective-permute-done((bf16[64,1280]{1,0:T(8,128)(2,1)}, bf16[64,1280]{1,0:T(8,128)(2,1)S(1)}, u32[]{:S(2)}, u32[]{:S(2)}) %collective-permute-start.2) | collective-permute-done | bytes 163872 | tf_op jit(solution)/shard_map/ppermute | solution.py:26
  11.4 1.7 %copy-done = bf16[8,2,16,5120]{3,2,1,0:T(8,128)(2,1)S(1)} copy-done((bf16[8,2,16,5120]{3,2,1,0:T(8,128)(2,1)S(1)}, bf16[8,2,16,5120]{3,2,1,0:T(8,128)(2,1)}, u32[]{:S(2)}) %copy-start) | copy-done | bytes 2621464
  14.7 1.6 %shrink.1 = bf16[2,64,256]{2,1,0:T(8,128)(2,1)S(1)} custom-call(s32[5]{0:T(128)S(1)} %stack.65.source_ref, s32[64,1]{1,0:T(8,128)S(1)} %copy.9.ids_ref, s32[1,32]{1,0:T(1,128)S(1)} %bitcast.117, bf16[64,64]{1,0:T(8,128)(2,1)S(1)} %fusion.185.order_ref, bf16[8,2,16,5120]{3,2,1,0:T(8,128)(2,1)S(1)} %copy-done, bf16[64,1280]{1,0:T(8,128)(2,1)S(1)} %copy-done.1, ...), custom_call_target="tpu_custom_call" | custom-call | flops 167772160 | bytes 2621440 | tf_op jit(solution)/shard_map/shrink/pallas_call | solution.py:56
  16.3 2.0 %fusion.105 = f32[64,1280]{1,0:T(8,128)S(1)} fusion(bf16[256,6400]{1,0:T(8,128)(2,1)} %bitcast.118, bf16[2,64,256]{2,1,0:T(8,128)(2,1)S(1)} %shrink.1), kind=kOutput, calls=%fused_computation.67 | convolution fusion | flops 42188800 | bytes 1015808 | tf_op jit(solution)/shard_map/dot_general | solution.py:17
  18.3 1.8 %fusion.103 = f32[64,1280]{1,0:T(8,128)S(1)} fusion(bf16[256,6400]{1,0:T(8,128)(2,1)} %bitcast.119, bf16[2,64,256]{2,1,0:T(8,128)(2,1)S(1)} %shrink.1), kind=kOutput, calls=%fused_computation.65 | convolution fusion | flops 42188800 | bytes 1015808 | tf_op jit(solution)/shard_map/dot_general | solution.py:17
  30.8 2.6 %fusion.96 = f32[1,64,1280]{2,1,0:T(8,128)S(1)} fusion(f32[64,1280]{1,0:T(8,128)S(1)} %fusion.105, bf16[64,1280]{1,0:T(8,128)(2,1)S(1)} %convolution_convert_fusion.1, bf16[1280,6400]{1,0:T(8,128)(2,1)} %param.10), kind=kOutput, calls=%fused_computation.62 | convolution fusion | flops 209797120 | bytes 4096000 | tf_op jit(solution)/shard_map/dot_general | solution.py:17
  34.3 2.6 %fusion.90 = f32[1,64,1280]{2,1,0:T(8,128)S(1)} fusion(f32[64,1280]{1,0:T(8,128)S(1)} %fusion.109, bf16[64,1280]{1,0:T(8,128)(2,1)S(1)} %convolution_convert_fusion.1, bf16[1280,6400]{1,0:T(8,128)(2,1)} %param.10), kind=kOutput, calls=%fused_computation.60 | convolution fusion | flops 209797120 | bytes 4096000 | tf_op jit(solution)/shard_map/dot_general | solution.py:17
  38.2 2.6 %fusion.84 = f32[1,64,1280]{2,1,0:T(8,128)S(1)} fusion(f32[64,1280]{1,0:T(8,128)S(1)} %fusion.113, bf16[64,1280]{1,0:T(8,128)(2,1)S(1)} %convolution_convert_fusion.1, bf16[1280,6400]{1,0:T(8,128)(2,1)} %param.10), kind=kOutput, calls=%fused_computation.58 | convolution fusion | flops 209797120 | bytes 4096000 | tf_op jit(solution)/shard_map/dot_general | solution.py:17
  41.7 2.6 %fusion.78 = f32[1,64,1280]{2,1,0:T(8,128)S(1)} fusion(f32[64,1280]{1,0:T(8,128)S(1)} %fusion.117, bf16[64,1280]{1,0:T(8,128)(2,1)S(1)} %convolution_convert_fusion.1, bf16[1280,6400]{1,0:T(8,128)(2,1)} %param.10), kind=kOutput, calls=%fused_computation.56 | convolution fusion | flops 209797120 | bytes 4096000 | tf_op jit(solution)/shard_map/dot_general | solution.py:17
  46.3 3.1 %fusion.72 = f32[1,64,1280]{2,1,0:T(8,128)S(1)} fusion(f32[64,1280]{1,0:T(8,128)S(1)} %fusion.121, bf16[64,1280]{1,0:T(8,128)(2,1)S(1)} %convolution_convert_fusion.1, bf16[1280,6400]{1,0:T(8,128)(2,1)} %param.10), kind=kOutput, calls=%fused_computation.54 | convolution fusion | flops 209797120 | bytes 4096000 | tf_op jit(solution)/shard_map/dot_general | solution.py:17
  49.8 1.6 %collective-permute-start.4 = (bf16[2,32,1280]{2,1,0:T(8,128)(2,1)S(1)}, bf16[2,32,1280]{2,1,0:T(8,128)(2,1)S(1)}, u32[]{:S(2)}, u32[]{:S(2)}) collective-permute-start(bf16[2,32,1280]{2,1,0:T(8,128)(2,1)S(1)} %fusion.204), channel_id=1, source_target_pairs={{8,0},{12,4},{0,8},{4,12},{9,1},{13,5},{1,9},{5,13},{10,2},{14,6},... | collective-permute-start | bytes 491528 | tf_op jit(solution)/shard_map/ppermute | solution.py:26
  52.1 1.6 %collective-permute-start.10 = (bf16[2,32,1280]{2,1,0:T(8,128)(2,1)S(1)}, bf16[2,32,1280]{2,1,0:T(8,128)(2,1)S(1)}, u32[]{:S(2)}, u32[]{:S(2)}) collective-permute-start(bf16[2,32,1280]{2,1,0:T(8,128)(2,1)S(1)} %fusion.206), channel_id=1, source_target_pairs={{8,0},{12,4},{0,8},{4,12},{9,1},{13,5},{1,9},{5,13},{10,2},{14,6},... | collective-permute-start | bytes 491528 | tf_op jit(solution)/shard_map/ppermute | solution.py:26
  54.3 1.6 %collective-permute-start.16 = (bf16[2,32,1280]{2,1,0:T(8,128)(2,1)S(1)}, bf16[2,32,1280]{2,1,0:T(8,128)(2,1)S(1)}, u32[]{:S(2)}, u32[]{:S(2)}) collective-permute-start(bf16[2,32,1280]{2,1,0:T(8,128)(2,1)S(1)} %fusion.208), channel_id=1, source_target_pairs={{8,0},{12,4},{0,8},{4,12},{9,1},{13,5},{1,9},{5,13},{10,2},{14,6},... | collective-permute-start | bytes 491528 | tf_op jit(solution)/shard_map/ppermute | solution.py:26
  57.2 3.3 %collective-permute-done.7 = bf16[2,32,1280]{2,1,0:T(8,128)(2,1)S(1)} collective-permute-done((bf16[2,32,1280]{2,1,0:T(8,128)(2,1)S(1)}, bf16[2,32,1280]{2,1,0:T(8,128)(2,1)S(1)}, u32[]{:S(2)}, u32[]{:S(2)}) %collective-permute-start.7) | collective-permute-done | bytes 163872 | tf_op jit(solution)/shard_map/ppermute | solution.py:26
  60.7 3.3 %collective-permute-done.10 = bf16[2,32,1280]{2,1,0:T(8,128)(2,1)S(1)} collective-permute-done((bf16[2,32,1280]{2,1,0:T(8,128)(2,1)S(1)}, bf16[2,32,1280]{2,1,0:T(8,128)(2,1)S(1)}, u32[]{:S(2)}, u32[]{:S(2)}) %collective-permute-start.10) | collective-permute-done | bytes 163872 | tf_op jit(solution)/shard_map/ppermute | solution.py:26
  64.2 3.3 %collective-permute-done.13 = bf16[2,32,1280]{2,1,0:T(8,128)(2,1)S(1)} collective-permute-done((bf16[2,32,1280]{2,1,0:T(8,128)(2,1)S(1)}, bf16[2,32,1280]{2,1,0:T(8,128)(2,1)S(1)}, u32[]{:S(2)}, u32[]{:S(2)}) %collective-permute-start.13) | collective-permute-done | bytes 163872 | tf_op jit(solution)/shard_map/ppermute | solution.py:26
  67.7 2.5 %collective-permute-done.16 = bf16[2,32,1280]{2,1,0:T(8,128)(2,1)S(1)} collective-permute-done((bf16[2,32,1280]{2,1,0:T(8,128)(2,1)S(1)}, bf16[2,32,1280]{2,1,0:T(8,128)(2,1)S(1)}, u32[]{:S(2)}, u32[]{:S(2)}) %collective-permute-start.16) | collective-permute-done | bytes 163872 | tf_op jit(solution)/shard_map/ppermute | solution.py:26
  74.1 1.7 %collective-permute-start.18 = (bf16[16,1280]{1,0:T(8,128)(2,1)S(1)}, bf16[16,1280]{1,0:T(8,128)(2,1)S(1)}, u32[]{:S(2)}, u32[]{:S(2)}) collective-permute-start(bf16[16,1280]{1,0:T(8,128)(2,1)S(1)} %get-tuple-element.5), channel_id=1, source_target_pairs={{0,1},{1,2},{2,3},{3,0},{4,5},{5,6},{6,7},{7,4},{8,9},{9,10},{10,1... | collective-permute-start | bytes 122888 | tf_op jit(solution)/shard_map/ppermute | solution.py:139
  75.8 2.6 %collective-permute-start.19 = (bf16[16,1280]{1,0:T(8,128)(2,1)S(1)}, bf16[16,1280]{1,0:T(8,128)(2,1)S(1)}, u32[]{:S(2)}, u32[]{:S(2)}) collective-permute-start(bf16[16,1280]{1,0:T(8,128)(2,1)S(1)} %get-tuple-element.7), channel_id=1, source_target_pairs={{0,2},{1,3},{2,0},{3,1},{4,6},{5,7},{6,4},{7,5},{8,10},{9,11},{10,... | collective-permute-start | bytes 122888 | tf_op jit(solution)/shard_map/ppermute | solution.py:139
  80.1 1.9 %collective-permute-done.19 = bf16[16,1280]{1,0:T(8,128)(2,1)S(1)} collective-permute-done((bf16[16,1280]{1,0:T(8,128)(2,1)S(1)}, bf16[16,1280]{1,0:T(8,128)(2,1)S(1)}, u32[]{:S(2)}, u32[]{:S(2)}) %collective-permute-start.19) | collective-permute-done | bytes 40992 | tf_op jit(solution)/shard_map/ppermute | solution.py:139
  82.5 3.2 %collective-permute-start.21 = (bf16[16,1280]{1,0:T(8,128)(2,1)S(1)}, bf16[16,1280]{1,0:T(8,128)(2,1)S(1)}, u32[]{:S(2)}, u32[]{:S(2)}) collective-permute-start(bf16[16,1280]{1,0:T(8,128)(2,1)S(1)} %fusion.181), channel_id=1, source_target_pairs={{1,0},{2,1},{3,2},{0,3},{5,4},{6,5},{7,6},{4,7},{9,8},{10,9},{11,1... | collective-permute-start | bytes 122888 | tf_op jit(solution)/shard_map/ppermute | solution.py:144
  87.3 3.2 %collective-permute-done.22 = bf16[16,1280]{1,0:T(8,128)(2,1)S(1)} collective-permute-done((bf16[16,1280]{1,0:T(8,128)(2,1)S(1)}, bf16[16,1280]{1,0:T(8,128)(2,1)S(1)}, u32[]{:S(2)}, u32[]{:S(2)}) %collective-permute-start.22) | collective-permute-done | bytes 40992 | tf_op jit(solution)/shard_map/ppermute | solution.py:144
  (101 shorter events, 33.0 us)
Async XLA Ops:
  0.0 5.2 %collective-permute-start = (bf16[64,1280]{1,0:T(8,128)(2,1)}, bf16[64,1280]{1,0:T(8,128)(2,1)S(1)}, u32[]{:S(2)}, u32[]{:S(2)}) collective-permute-start(bf16[64,1280]{1,0:T(8,128)(2,1)} %refs_0_.1), channel_id=1, source_target_pairs={{0,4},{4,0},{8,12},{12,8},{1,5},{5,1},{9,13},{13,9},{2,6},{6,2},{1... | collective-permute-start | bytes 491528 | tf_op jit(solution)/shard_map/ppermute | solution.py:21
  0.5 7.8 %collective-permute-start.1 = (bf16[64,1280]{1,0:T(8,128)(2,1)}, bf16[64,1280]{1,0:T(8,128)(2,1)S(1)}, u32[]{:S(2)}, u32[]{:S(2)}) collective-permute-start(bf16[64,1280]{1,0:T(8,128)(2,1)} %refs_0_.1), channel_id=1, source_target_pairs={{8,0},{12,4},{0,8},{4,12},{9,1},{13,5},{1,9},{5,13},{10,2},{14,6},... | collective-permute-start | bytes 491528 | tf_op jit(solution)/shard_map/ppermute | solution.py:26
  3.0 8.4 %collective-permute-start.2 = (bf16[64,1280]{1,0:T(8,128)(2,1)}, bf16[64,1280]{1,0:T(8,128)(2,1)S(1)}, u32[]{:S(2)}, u32[]{:S(2)}) collective-permute-start(bf16[64,1280]{1,0:T(8,128)(2,1)} %refs_0_.1), channel_id=1, source_target_pairs={{12,0},{8,4},{4,8},{0,12},{13,1},{9,5},{5,9},{1,13},{14,2},{10,6},... | collective-permute-start | bytes 491528 | tf_op jit(solution)/shard_map/ppermute | solution.py:26
  34.1 15.7 %collective-permute-start.3 = (bf16[2,32,1280]{2,1,0:T(8,128)(2,1)S(1)}, bf16[2,32,1280]{2,1,0:T(8,128)(2,1)S(1)}, u32[]{:S(2)}, u32[]{:S(2)}) collective-permute-start(bf16[2,32,1280]{2,1,0:T(8,128)(2,1)S(1)} %fusion.146), channel_id=1, source_target_pairs={{0,4},{4,0},{8,12},{12,8},{1,5},{5,1},{9,13},{13,9},{2,6},{6,2},{1... | collective-permute-start | bytes 491528 | tf_op jit(solution)/shard_map/ppermute | solution.py:21
  37.7 13.8 %collective-permute-start.6 = (bf16[2,32,1280]{2,1,0:T(8,128)(2,1)S(1)}, bf16[2,32,1280]{2,1,0:T(8,128)(2,1)S(1)}, u32[]{:S(2)}, u32[]{:S(2)}) collective-permute-start(bf16[2,32,1280]{2,1,0:T(8,128)(2,1)S(1)} %fusion.145), channel_id=1, source_target_pairs={{0,4},{4,0},{8,12},{12,8},{1,5},{5,1},{9,13},{13,9},{2,6},{6,2},{1... | collective-permute-start | bytes 491528 | tf_op jit(solution)/shard_map/ppermute | solution.py:21
  41.5 10.5 %collective-permute-start.9 = (bf16[2,32,1280]{2,1,0:T(8,128)(2,1)S(1)}, bf16[2,32,1280]{2,1,0:T(8,128)(2,1)S(1)}, u32[]{:S(2)}, u32[]{:S(2)}) collective-permute-start(bf16[2,32,1280]{2,1,0:T(8,128)(2,1)S(1)} %fusion.144), channel_id=1, source_target_pairs={{0,4},{4,0},{8,12},{12,8},{1,5},{5,1},{9,13},{13,9},{2,6},{6,2},{1... | collective-permute-start | bytes 491528 | tf_op jit(solution)/shard_map/ppermute | solution.py:21
  45.1 8.6 %collective-permute-start.12 = (bf16[2,32,1280]{2,1,0:T(8,128)(2,1)S(1)}, bf16[2,32,1280]{2,1,0:T(8,128)(2,1)S(1)}, u32[]{:S(2)}, u32[]{:S(2)}) collective-permute-start(bf16[2,32,1280]{2,1,0:T(8,128)(2,1)S(1)} %fusion.143), channel_id=1, source_target_pairs={{0,4},{4,0},{8,12},{12,8},{1,5},{5,1},{9,13},{13,9},{2,6},{6,2},{1... | collective-permute-start | bytes 491528 | tf_op jit(solution)/shard_map/ppermute | solution.py:21
  49.4 4.9 %collective-permute-start.15 = (bf16[2,32,1280]{2,1,0:T(8,128)(2,1)S(1)}, bf16[2,32,1280]{2,1,0:T(8,128)(2,1)S(1)}, u32[]{:S(2)}, u32[]{:S(2)}) collective-permute-start(bf16[2,32,1280]{2,1,0:T(8,128)(2,1)S(1)} %fusion.142), channel_id=1, source_target_pairs={{0,4},{4,0},{8,12},{12,8},{1,5},{5,1},{9,13},{13,9},{2,6},{6,2},{1... | collective-permute-start | bytes 491528 | tf_op jit(solution)/shard_map/ppermute | solution.py:21
  49.8 7.1 %collective-permute-start.4 = (bf16[2,32,1280]{2,1,0:T(8,128)(2,1)S(1)}, bf16[2,32,1280]{2,1,0:T(8,128)(2,1)S(1)}, u32[]{:S(2)}, u32[]{:S(2)}) collective-permute-start(bf16[2,32,1280]{2,1,0:T(8,128)(2,1)S(1)} %fusion.204), channel_id=1, source_target_pairs={{8,0},{12,4},{0,8},{4,12},{9,1},{13,5},{1,9},{5,13},{10,2},{14,6},... | collective-permute-start | bytes 491528 | tf_op jit(solution)/shard_map/ppermute | solution.py:26
  51.5 9.0 %collective-permute-start.7 = (bf16[2,32,1280]{2,1,0:T(8,128)(2,1)S(1)}, bf16[2,32,1280]{2,1,0:T(8,128)(2,1)S(1)}, u32[]{:S(2)}, u32[]{:S(2)}) collective-permute-start(bf16[2,32,1280]{2,1,0:T(8,128)(2,1)S(1)} %fusion.205), channel_id=1, source_target_pairs={{8,0},{12,4},{0,8},{4,12},{9,1},{13,5},{1,9},{5,13},{10,2},{14,6},... | collective-permute-start | bytes 491528 | tf_op jit(solution)/shard_map/ppermute | solution.py:26
  52.1 11.9 %collective-permute-start.10 = (bf16[2,32,1280]{2,1,0:T(8,128)(2,1)S(1)}, bf16[2,32,1280]{2,1,0:T(8,128)(2,1)S(1)}, u32[]{:S(2)}, u32[]{:S(2)}) collective-permute-start(bf16[2,32,1280]{2,1,0:T(8,128)(2,1)S(1)} %fusion.206), channel_id=1, source_target_pairs={{8,0},{12,4},{0,8},{4,12},{9,1},{13,5},{1,9},{5,13},{10,2},{14,6},... | collective-permute-start | bytes 491528 | tf_op jit(solution)/shard_map/ppermute | solution.py:26
  53.7 13.8 %collective-permute-start.13 = (bf16[2,32,1280]{2,1,0:T(8,128)(2,1)S(1)}, bf16[2,32,1280]{2,1,0:T(8,128)(2,1)S(1)}, u32[]{:S(2)}, u32[]{:S(2)}) collective-permute-start(bf16[2,32,1280]{2,1,0:T(8,128)(2,1)S(1)} %fusion.207), channel_id=1, source_target_pairs={{8,0},{12,4},{0,8},{4,12},{9,1},{13,5},{1,9},{5,13},{10,2},{14,6},... | collective-permute-start | bytes 491528 | tf_op jit(solution)/shard_map/ppermute | solution.py:26
  54.3 15.9 %collective-permute-start.16 = (bf16[2,32,1280]{2,1,0:T(8,128)(2,1)S(1)}, bf16[2,32,1280]{2,1,0:T(8,128)(2,1)S(1)}, u32[]{:S(2)}, u32[]{:S(2)}) collective-permute-start(bf16[2,32,1280]{2,1,0:T(8,128)(2,1)S(1)} %fusion.208), channel_id=1, source_target_pairs={{8,0},{12,4},{0,8},{4,12},{9,1},{13,5},{1,9},{5,13},{10,2},{14,6},... | collective-permute-start | bytes 491528 | tf_op jit(solution)/shard_map/ppermute | solution.py:26
  57.1 16.2 %collective-permute-start.5 = (bf16[32,1280]{1,0:T(8,128)(2,1)S(1)}, bf16[32,1280]{1,0:T(8,128)(2,1)S(1)}, u32[]{:S(2)}, u32[]{:S(2)}) collective-permute-start(bf16[32,1280]{1,0:T(8,128)(2,1)S(1)} %fusion.156), channel_id=1, source_target_pairs={{0,4},{4,0},{8,12},{12,8},{1,5},{5,1},{9,13},{13,9},{2,6},{6,2},{1... | collective-permute-start | bytes 245768 | tf_op jit(solution)/shard_map/ppermute | solution.py:21
  60.6 9.8 %collective-permute-start.8 = (bf16[32,1280]{1,0:T(8,128)(2,1)S(1)}, bf16[32,1280]{1,0:T(8,128)(2,1)S(1)}, u32[]{:S(2)}, u32[]{:S(2)}) collective-permute-start(bf16[32,1280]{1,0:T(8,128)(2,1)S(1)} %fusion.154), channel_id=1, source_target_pairs={{0,4},{4,0},{8,12},{12,8},{1,5},{5,1},{9,13},{13,9},{2,6},{6,2},{1... | collective-permute-start | bytes 245768 | tf_op jit(solution)/shard_map/ppermute | solution.py:21
  64.1 7.1 %collective-permute-start.11 = (bf16[32,1280]{1,0:T(8,128)(2,1)S(1)}, bf16[32,1280]{1,0:T(8,128)(2,1)S(1)}, u32[]{:S(2)}, u32[]{:S(2)}) collective-permute-start(bf16[32,1280]{1,0:T(8,128)(2,1)S(1)} %fusion.152), channel_id=1, source_target_pairs={{0,4},{4,0},{8,12},{12,8},{1,5},{5,1},{9,13},{13,9},{2,6},{6,2},{1... | collective-permute-start | bytes 245768 | tf_op jit(solution)/shard_map/ppermute | solution.py:21
  67.6 4.2 %collective-permute-start.14 = (bf16[32,1280]{1,0:T(8,128)(2,1)S(1)}, bf16[32,1280]{1,0:T(8,128)(2,1)S(1)}, u32[]{:S(2)}, u32[]{:S(2)}) collective-permute-start(bf16[32,1280]{1,0:T(8,128)(2,1)S(1)} %fusion.150), channel_id=1, source_target_pairs={{0,4},{4,0},{8,12},{12,8},{1,5},{5,1},{9,13},{13,9},{2,6},{6,2},{1... | collective-permute-start | bytes 245768 | tf_op jit(solution)/shard_map/ppermute | solution.py:21
  70.3 2.3 %collective-permute-start.17 = (bf16[32,1280]{1,0:T(8,128)(2,1)S(1)}, bf16[32,1280]{1,0:T(8,128)(2,1)S(1)}, u32[]{:S(2)}, u32[]{:S(2)}) collective-permute-start(bf16[32,1280]{1,0:T(8,128)(2,1)S(1)} %fusion.148), channel_id=1, source_target_pairs={{0,4},{4,0},{8,12},{12,8},{1,5},{5,1},{9,13},{13,9},{2,6},{6,2},{1... | collective-permute-start | bytes 245768 | tf_op jit(solution)/shard_map/ppermute | solution.py:21
  74.1 6.0 %collective-permute-start.18 = (bf16[16,1280]{1,0:T(8,128)(2,1)S(1)}, bf16[16,1280]{1,0:T(8,128)(2,1)S(1)}, u32[]{:S(2)}, u32[]{:S(2)}) collective-permute-start(bf16[16,1280]{1,0:T(8,128)(2,1)S(1)} %get-tuple-element.5), channel_id=1, source_target_pairs={{0,1},{1,2},{2,3},{3,0},{4,5},{5,6},{6,7},{7,4},{8,9},{9,10},{10,1... | collective-permute-start | bytes 122888 | tf_op jit(solution)/shard_map/ppermute | solution.py:139
  75.8 6.2 %collective-permute-start.19 = (bf16[16,1280]{1,0:T(8,128)(2,1)S(1)}, bf16[16,1280]{1,0:T(8,128)(2,1)S(1)}, u32[]{:S(2)}, u32[]{:S(2)}) collective-permute-start(bf16[16,1280]{1,0:T(8,128)(2,1)S(1)} %get-tuple-element.7), channel_id=1, source_target_pairs={{0,2},{1,3},{2,0},{3,1},{4,6},{5,7},{6,4},{7,5},{8,10},{9,11},{10,... | collective-permute-start | bytes 122888 | tf_op jit(solution)/shard_map/ppermute | solution.py:139
  78.4 4.0 %collective-permute-start.20 = (bf16[16,1280]{1,0:T(8,128)(2,1)S(1)}, bf16[16,1280]{1,0:T(8,128)(2,1)S(1)}, u32[]{:S(2)}, u32[]{:S(2)}) collective-permute-start(bf16[16,1280]{1,0:T(8,128)(2,1)S(1)} %get-tuple-element.6), channel_id=1, source_target_pairs={{0,3},{1,0},{2,1},{3,2},{4,7},{5,4},{6,5},{7,6},{8,11},{9,8},{10,9... | collective-permute-start | bytes 122888 | tf_op jit(solution)/shard_map/ppermute | solution.py:139
  82.5 4.8 %collective-permute-start.21 = (bf16[16,1280]{1,0:T(8,128)(2,1)S(1)}, bf16[16,1280]{1,0:T(8,128)(2,1)S(1)}, u32[]{:S(2)}, u32[]{:S(2)}) collective-permute-start(bf16[16,1280]{1,0:T(8,128)(2,1)S(1)} %fusion.181), channel_id=1, source_target_pairs={{1,0},{2,1},{3,2},{0,3},{5,4},{6,5},{7,6},{4,7},{9,8},{10,9},{11,1... | collective-permute-start | bytes 122888 | tf_op jit(solution)/shard_map/ppermute | solution.py:144
  85.6 4.9 %collective-permute-start.22 = (bf16[16,1280]{1,0:T(8,128)(2,1)S(1)}, bf16[16,1280]{1,0:T(8,128)(2,1)S(1)}, u32[]{:S(2)}, u32[]{:S(2)}) collective-permute-start(bf16[16,1280]{1,0:T(8,128)(2,1)S(1)} %fusion.181), channel_id=1, source_target_pairs={{2,0},{3,1},{0,2},{1,3},{6,4},{7,5},{4,6},{5,7},{10,8},{11,9},{8,1... | collective-permute-start | bytes 122888 | tf_op jit(solution)/shard_map/ppermute | solution.py:144
  85.7 5.8 %collective-permute-start.23 = (bf16[16,1280]{1,0:T(8,128)(2,1)S(1)}, bf16[16,1280]{1,0:T(8,128)(2,1)S(1)}, u32[]{:S(2)}, u32[]{:S(2)}) collective-permute-start(bf16[16,1280]{1,0:T(8,128)(2,1)S(1)} %fusion.181), channel_id=1, source_target_pairs={{3,0},{0,1},{1,2},{2,3},{7,4},{4,5},{5,6},{6,7},{11,8},{8,9},{9,10... | collective-permute-start | bytes 122888 | tf_op jit(solution)/shard_map/ppermute | solution.py:144
  (8 other events, 104.0 us)

commit v2 on v1

v2 whole, which is shorter than its diff:
```python
import functools

import jax
import jax.numpy as jnp
from jax import lax
from jax.experimental import pallas as pl
from jax.experimental.pallas import tpu as pltpu
from jax.sharding import PartitionSpec as P

low_rank_scale = 0.5
f32 = jnp.float32
bf16 = jnp.bfloat16
MIB = 1 << 20
CHUNKS = (1280, 1280, 1280, 1280, 1280)
TILE = 640


def dot(a, b):
    return jnp.dot(a, b, preferred_element_type=f32)


def core_swap(value, replicas):
    return lax.ppermute(value, "replica", [(i, i ^ 1) for i in range(replicas)])


def from_chip(value, replicas, step, flip=0):
    pairs = [((i + 2 * step) % replicas ^ flip, i) for i in range(replicas)]
    return lax.ppermute(value, "replica", pairs)


def row_order(rows, block, chips, me, transposed=False):
    mine = lax.broadcasted_iota(jnp.int32, (rows, rows), 1 if transposed else 0)
    batch = lax.broadcasted_iota(jnp.int32, (rows, rows), 0 if transposed else 1)
    nth = mine // block
    chip = (me // 2 + nth % chips) % chips
    core = (me % 2 + nth // chips) % 2
    return (batch == (chip * 2 + core) * block + mine % block).astype(f32).astype(bf16)


def widen_into(spread, expand_ref, base_ref, start, width, own_ref, away_ref):
    half = own_ref.shape[1]
    rows = 2 * half
    delta = dot(spread, expand_ref[:, start : start + width])
    delta = (low_rank_scale * delta).astype(bf16).astype(f32)
    for p in range(2):
        total = base_ref[p, :, start : start + width] + delta[p * rows : (p + 1) * rows]
        own_ref[p] = total[:half]
        away_ref[p] = total[half:].astype(bf16)


def shrink_kernel(block, sources, ids_ref, slots_ref, down_ref, expand_ref, base_ref, *refs):
    pieces, (spread_ref, own_ref, away_ref) = refs[:-3], refs[-3:]
    me = lax.axis_index("replica")
    rows, width = pieces[0].shape
    stored, _, rank, _ = down_ref.shape
    table = stored * 2 * rank
    total = jnp.zeros((rows, table), f32)
    for piece, source in zip(pieces, sources(me)):
        columns = pl.ds(pl.multiple_of(source * width, 128), width)
        part = down_ref[:, :, :, columns].reshape(table, width)
        total += lax.dot_general(piece[...], part, (((1,), (1,)), ((), ())), preferred_element_type=f32)
    shrink = total.astype(bf16).astype(f32)
    adapters = slots_ref.shape[1]
    known = lax.broadcasted_iota(jnp.int32, (adapters, rows), 0)
    chosen = (known == ids_ref[...]).astype(f32).astype(bf16)
    slots = jnp.broadcast_to(slots_ref[...].astype(f32), (table, adapters)).astype(bf16)
    slot = lax.dot_general(chosen, slots, (((0,), (1,)), ((), ())), preferred_element_type=f32)
    first = (slot.astype(jnp.int32) - me * stored) * (2 * rank)
    column = lax.broadcasted_iota(jnp.int32, (rows, table), 1)
    order = row_order(rows, block, len(pieces) // 2, me)
    for p in range(2):
        begin = first + p * rank
        mine = jnp.logical_and(column >= begin, column < begin + rank)
        picked = jnp.where(mine, shrink, 0.0).astype(bf16)
        spread_ref[p * rows : (p + 1) * rows] = dot(order, picked).astype(bf16)
    widen_into(spread_ref[...], expand_ref, base_ref, 0, own_ref.shape[2], own_ref, away_ref)


def parted(half, width):
    return [jax.ShapeDtypeStruct((2, half, width), f32), jax.ShapeDtypeStruct((2, half, width), bf16)]


def shrink_rows(pieces, sources, block, ids, slots, adapter_down, expand, base, width):
    rows = ids.shape[0]
    vmem = pl.BlockSpec(memory_space=pltpu.VMEM)
    return pl.pallas_call(
        functools.partial(shrink_kernel, block, sources),
        out_shape=[jax.ShapeDtypeStruct((2 * rows, expand.shape[0]), bf16)] + parted(rows // 2, width),
        in_specs=[vmem] * (5 + len(pieces)),
        out_specs=[vmem] * 3,
        compiler_params=pltpu.CompilerParams(vmem_limit_bytes=(16 if rows <= 64 else 40) * MIB),
        cost_estimate=pl.CostEstimate(
            flops=2 * adapter_down.size * rows, bytes_accessed=2 * adapter_down.size, transcendentals=0
        ),
        name="shrink",
    )(ids.reshape(1, rows), slots.reshape(1, -1), adapter_down, expand, base, *pieces)


def widen_kernel(widths, start, spread_ref, expand_ref, base_ref, *out_refs):
    for k, width in enumerate(widths):
        widen_into(spread_ref[...], expand_ref, base_ref, start, width, out_refs[2 * k], out_refs[2 * k + 1])
        start += width


def widen(spread, expand, base, start, widths):
    half = spread.shape[0] // 4
    vmem = pl.BlockSpec(memory_space=pltpu.VMEM)
    return pl.pallas_call(
        functools.partial(widen_kernel, widths, start),
        out_shape=[shape for width in widths for shape in parted(half, width)],
        in_specs=[vmem] * 3,
        out_specs=[vmem] * (2 * len(widths)),
        compiler_params=pltpu.CompilerParams(vmem_limit_bytes=16 * MIB),
        cost_estimate=pl.CostEstimate(
            flops=2 * spread.size * sum(widths), bytes_accessed=4 * spread.size, transcendentals=0
        ),
        name="widen",
    )(spread, expand, base)


def stream_kernel(block, chips, tile, x_ref, gate_ref, up_ref, out_ref, mixed, held, arrived):
    slots = held.shape[0]
    rows = x_ref.shape[0]
    work = [(p, at) for at in range(0, gate_ref.shape[1], tile) for p in range(2)]

    def fetch(i):
        p, at = work[i]
        source = (gate_ref, up_ref)[p].at[:, pl.ds(at, tile)]
        return pltpu.make_async_copy(source, held.at[i % slots], arrived.at[i % slots])

    for i in range(min(slots, len(work))):
        fetch(i).start()
    order = row_order(rows, block, chips, lax.axis_index("replica"))
    mixed[...] = dot(order, x_ref[...]).astype(bf16)
    for i, (p, at) in enumerate(work):
        fetch(i).wait()
        out_ref[p, :, at : at + tile] = dot(mixed[...], held[i % slots])
        if i + slots < len(work):
            fetch(i + slots).start()


def stream(x, gate, up, block, chips, tile, slots=8):
    rows, depth = x.shape
    width = gate.shape[1]
    vmem = pl.BlockSpec(memory_space=pltpu.VMEM)
    far = pl.BlockSpec(memory_space=pltpu.HBM)
    return pl.pallas_call(
        functools.partial(stream_kernel, block, chips, tile),
        out_shape=jax.ShapeDtypeStruct((2, rows, width), f32),
        in_specs=[vmem, far, far],
        out_specs=vmem,
        scratch_shapes=[
            pltpu.VMEM((rows, depth), bf16),
            pltpu.VMEM((slots, depth, tile), bf16),
            pltpu.SemaphoreType.DMA((slots,)),
        ],
        compiler_params=pltpu.CompilerParams(vmem_limit_bytes=50 * MIB),
        cost_estimate=pl.CostEstimate(
            flops=4 * rows * depth * width, bytes_accessed=4 * depth * width, transcendentals=0
        ),
        name="stream",
    )(x, gate, up)


def join_kernel(own_ref, got_ref, sum_ref, send_ref):
    total = own_ref[...] + got_ref[...].astype(f32)
    sum_ref[...] = total
    send_ref[...] = total.astype(bf16)


def join(own, got):
    vmem = pl.BlockSpec(memory_space=pltpu.VMEM)
    return pl.pallas_call(
        join_kernel,
        out_shape=[jax.ShapeDtypeStruct(own.shape, f32), jax.ShapeDtypeStruct(own.shape, bf16)],
        in_specs=[vmem] * 2,
        out_specs=[vmem] * 2,
        compiler_params=pltpu.CompilerParams(vmem_limit_bytes=8 * MIB),
        cost_estimate=pl.CostEstimate(flops=1, bytes_accessed=1, transcendentals=0),
        name="join",
    )(own, got)


def activate_kernel(block, own_ref, *refs):
    hidden_ref = refs[-1]
    half = own_ref.shape[1]

    def total(p, lo):
        sums = own_ref[p, lo : lo + block]
        for step, got_ref in enumerate(refs[:-1], 1):
            at = (lo - step * block) % half
            sums += got_ref[p, at : at + block].astype(f32)
        return sums

    for lo in range(0, half, block):
        gate, up = total(0, lo), total(1, lo)
        hidden_ref[lo : lo + block] = (gate / (1.0 + jnp.exp(-gate)) * up).astype(bf16)


def activate(block, own, gots):
    vmem = pl.BlockSpec(memory_space=pltpu.VMEM)
    return pl.pallas_call(
        functools.partial(activate_kernel, block),
        out_shape=jax.ShapeDtypeStruct(own.shape[1:], bf16),
        in_specs=[vmem] * (1 + len(gots)),
        out_specs=vmem,
        compiler_params=pltpu.CompilerParams(vmem_limit_bytes=8 * MIB),
        cost_estimate=pl.CostEstimate(flops=1, bytes_accessed=1, transcendentals=0),
        name="activate",
    )(own, *gots)


def project_kernel(start, own_ref, got_ref, down_ref, *refs):
    total_ref, hidden, held, arrived = refs[-4:]
    half = own_ref.shape[0]
    pieces, depth, _ = held.shape

    def fetch(i):
        source = down_ref.at[pl.ds(start + i * depth, depth)]
        return pltpu.make_async_copy(source, held.at[i], arrived.at[i])

    for i in range(pieces):
        fetch(i).start()
    hidden[:half] = own_ref[...]
    hidden[half:] = got_ref[...]
    total = refs[0][...] if len(refs) > 4 else jnp.zeros(total_ref.shape, f32)
    for i in range(pieces):
        fetch(i).wait()
        total += dot(hidden[:, i * depth : (i + 1) * depth], held[i])
    total_ref[...] = total


def project(start, own, got, down, total, depth=256):
    half, width = own.shape
    depth = depth if width % depth == 0 else 128
    rows, columns = 2 * half, down.shape[1]
    vmem = pl.BlockSpec(memory_space=pltpu.VMEM)
    before = [] if total is None else [total]
    return pl.pallas_call(
        functools.partial(project_kernel, start),
        out_shape=jax.ShapeDtypeStruct((rows, columns), f32),
        in_specs=[vmem] * 2 + [pl.BlockSpec(memory_space=pltpu.HBM)] + [vmem] * len(before),
        out_specs=vmem,
        scratch_shapes=[
            pltpu.VMEM((rows, width), bf16),
            pltpu.VMEM((width // depth, depth, columns), bf16),
            pltpu.SemaphoreType.DMA((width // depth,)),
        ],
        compiler_params=pltpu.CompilerParams(vmem_limit_bytes=50 * MIB),
        cost_estimate=pl.CostEstimate(flops=1, bytes_accessed=1, transcendentals=0),
        name="project",
    )(own, got, down, *before)


def shards(
    tokens, gate_matrix, up_matrix, down_weight, adapter_down, adapter_up, adapter_ids, adapter_slot
):
    replicas, depth = lax.axis_size("replica"), lax.axis_size("tensor")
    chips = replicas // 2
    layer = lax.axis_index("tensor")
    rows = tokens.shape[0]
    block = rows // replicas
    half = rows // 2
    units = gate_matrix.shape[1]

    pieces = [tokens, core_swap(tokens, replicas)]
    for step in range(1, chips):
        for flip in range(2):
            pieces.append(from_chip(tokens, replicas, step, flip))

    def sources(me):
        far = [((me + 2 * step) % replicas, flip) for step in range(1, chips) for flip in range(2)]
        near = [(me, 0), (me, 1)]
        return [at + flip * (1 - 2 * (at % 2)) for at, flip in near + far]

    widths = CHUNKS if sum(CHUNKS) == units else (units,)
    base = stream(tokens, gate_matrix, up_matrix, block, chips, TILE)
    expand = adapter_up.reshape(-1, units)
    spread, own, away = shrink_rows(
        pieces, sources, block, adapter_ids, adapter_slot, adapter_down, expand, base, widths[0]
    )
    parts = [own, away]
    if len(widths) > 1:
        parts += widen(spread, expand, base, widths[0], widths[1:])
    swapped = [core_swap(away, replicas) for away in parts[1::2]]
    joined = [join(own, got) for own, got in zip(parts[::2], swapped)]
    gots = [[from_chip(away, replicas, step) for step in range(1, chips)] for _, away in joined]
    total = None
    start = 0
    for width, (own, _), got in zip(widths, joined, gots):
        if total is not None:
            total, *got = lax.optimization_barrier((total, *got))
        hidden = activate(block, own, got)
        total = project(start, hidden, core_swap(hidden, replicas), down_weight, total)
        start += width

    share = rows // depth
    blocks = total.reshape(depth, share, -1)
    pick = [lax.dynamic_index_in_dim(blocks, (layer + s) % depth, 0, False) for s in range(depth)]
    mine = pick[0]
    for s in range(1, depth):
        pairs = [(i, (i + s) % depth) for i in range(depth)]
        mine = mine + lax.ppermute(pick[s].astype(bf16), "tensor", pairs).astype(f32)
    mine = mine.astype(bf16)
    got = [mine]
    for s in range(1, depth):
        pairs = [((i + s) % depth, i) for i in range(depth)]
        got.append(lax.ppermute(mine, "tensor", pairs))
    place = jnp.arange(rows, dtype=jnp.int32)
    held = (layer + place // share) % depth * share + place % share
    gather = (held[:, None] == place[None, :]).astype(bf16)
    order = row_order(rows, block, chips, lax.axis_index("replica"), True)
    back = dot(order, gather.T).astype(bf16)
    return dot(back, jnp.concatenate(got, axis=0)).astype(bf16)


def solution(mesh):
    placed = (
        P("groups", "replica"),
        P("replica", "tensor"),
        P("replica", "tensor"),
        P("tensor", "replica"),
        P("replica", None, None, None),
        P("replica", None, None, "tensor"),
        P("groups"),
        P("groups"),
    )
    return jax.shard_map(
        shards, mesh=mesh, in_specs=placed, out_specs=P("groups", "replica"), check_vma=False
    )
```

time: 93.2 us -> 63.2 us (0.68)
  matrix products: 37.3 us -> 1.04 us
  Pallas kernels: 1.61 us -> 25 us
  waiting for transfers between devices: 27.3 us -> 14.6 us
  local copies, waits for them, and re-layouts: 4.32 us -> 0.99 us
    dot_general x27 -> x1, matrix products: 37.3 us -> 1.04 us  [dot(): return jnp.dot(a, b, preferred_element_type=f32)]
    pallas_call x1 -> x18, Pallas kernels: 1.61 us -> 25 us  [the longest x1 11.3 us: stream(): pl.pallas_call(functools.partial(stream_kernel, block, chips, tile), out_...]
    ppermute x7, waiting for transfers between devices: 19.5 us -> 4.36 us  [from_chip(): return lax.ppermute(value, 'replica', pairs)]
    unnamed x16 -> x10, local copies, waits for them, and re-layouts: 3.34 us -> 0.96 us
    ppermute x11, waiting for transfers between devices: 0.04 us -> 2.4 us  [core_swap(): return lax.ppermute(value, 'replica', [(i, i ^ 1) for i in range(replicas)])]
  transfers between devices with their start and end apart: 24 -> 24, of which waited for: 13 -> 11; matrix products, arithmetic and copies ran while one was open for 21% -> 0% of each run, Pallas kernels for 0% -> 34%
where the time goes in v2:
time: 63.2 us; the launch traced here: 63 us
  Pallas kernels  25 us (40%)
  starting transfers between devices  21.1 us (33%)
  waiting for transfers between devices  14.6 us (23%)
  matrix products  1.04 us (2%)
  local copies, waits for them, and re-layouts  0.99 us (2%)
    pallas_call x1, Pallas kernels, stream(): pl.pallas_call(functools.partial(stream_kernel, block, chips, tile), out_...  11.3 us
    pallas_call x5, Pallas kernels, project(): pl.pallas_call(functools.partial(project_kernel, start), out_shape=jax.Sh...  11.1 us
    ppermute x7, starting transfers between devices, from_chip(): return lax.ppermute(value, 'replica', pairs)  8.88 us
    ppermute x3, starting transfers between devices, shards(): lax.ppermute(pick[s].astype(bf16), 'tensor', pairs).astype(f32)  5.56 us
    ppermute x3, waiting for transfers between devices, shards(): got.append(lax.ppermute(mine, 'tensor', pairs))  5.15 us
    ppermute x7, waiting for transfers between devices, from_chip(): return lax.ppermute(value, 'replica', pairs)  4.36 us
    ppermute x3, starting transfers between devices, shards(): got.append(lax.ppermute(mine, 'tensor', pairs))  3.82 us
    ppermute x11, starting transfers between devices, core_swap(): return lax.ppermute(value, 'replica', [(i, i ^ 1) for i in range(replicas)])  2.83 us
  transfers between devices with their start and end apart: 24, of which 11 were waited for; matrix products, arithmetic and copies ran while one was open for 0% of the time, Pallas kernels for 34%

profile of v2, /device:TPU:0, one launch (start us, length us, event | category | flops | bytes accessed | tf_op | source)
XLA Modules:
  0.0 63.0 jit_solution(5632148376303941727)
XLA Ops:
  0.5 2.6 %collective-permute-start.1 = (bf16[64,1280]{1,0:T(8,128)(2,1)}, bf16[64,1280]{1,0:T(8,128)(2,1)S(1)}, u32[]{:S(2)}, u32[]{:S(2)}) collective-permute-start(bf16[64,1280]{1,0:T(8,128)(2,1)} %refs_0_.1), channel_id=1, source_target_pairs={{8,0},{12,4},{0,8},{4,12},{9,1},{13,5},{1,9},{5,13},{10,2},{14,6},... | collective-permute-start | bytes 491528 | tf_op jit(solution)/shard_map/ppermute | solution.py:28
  3.1 0.9 %copy-done.2 = bf16[64,1280]{1,0:T(8,128)(2,1)S(1)} copy-done((bf16[64,1280]{1,0:T(8,128)(2,1)S(1)}, bf16[64,1280]{1,0:T(8,128)(2,1)}, u32[]{:S(2)}) %copy-start.2) | copy-done | bytes 163864
  4.1 11.3 %stream.1.base_ref = f32[2,64,6400]{2,1,0:T(8,128)S(1)} custom-call(bf16[64,1280]{1,0:T(8,128)(2,1)S(1)} %copy-done.2, bf16[1280,6400]{1,0:T(8,128)(2,1)} %gate_ref.1, bf16[1280,6400]{1,0:T(8,128)(2,1)} %up_ref.1), custom_call_target="tpu_custom_call" | custom-call | flops 2097152000 | bytes 32768000 | tf_op jit(solution)/shard_map/stream/pallas_call | solution.py:147
  15.5 1.5 %shrink.1 = (bf16[128,256]{1,0:T(8,128)(2,1)S(1)}, f32[2,32,1280]{2,1,0:T(8,128)S(1)}, bf16[2,32,1280]{2,1,0:T(8,128)(2,1)S(1)}) custom-call(s32[1,64]{1,0:T(1,128)S(1)} %bitcast.22, s32[1,32]{1,0:T(1,128)S(1)} %bitcast.23, bf16[8,2,16,5120]{3,2,1,0:T(8,128)(2,1)S(1)} %copy-done.1, bf16[256,6400]{1,0:T(8,128)(2,1)S(1)} %bitcast.18, ...), custom_call_target="tpu_custom_call" | custom-call | flops 167772160 | bytes 2621440 | tf_op jit(solution)/shard_map/shrink/pallas_call | solution.py:86
  18.5 1.8 %collective-permute-start.8 = (bf16[2,32,1280]{2,1,0:T(8,128)(2,1)S(1)}, bf16[2,32,1280]{2,1,0:T(8,128)(2,1)S(1)}, u32[]{:S(2)}, u32[]{:S(2)}) collective-permute-start(bf16[2,32,1280]{2,1,0:T(8,128)(2,1)S(1)} %get-tuple-element.50), channel_id=1, source_target_pairs={{8,0},{12,4},{0,8},{4,12},{9,1},{13,5},{1,9},{5,13},{10,2},{14,6},... | collective-permute-start | bytes 491528 | tf_op jit(solution)/shard_map/ppermute | solution.py:28
  21.2 4.3 %collective-permute-done.8.refs_0_ = bf16[2,32,1280]{2,1,0:T(8,128)(2,1)S(1)} collective-permute-done((bf16[2,32,1280]{2,1,0:T(8,128)(2,1)S(1)}, bf16[2,32,1280]{2,1,0:T(8,128)(2,1)S(1)}, u32[]{:S(2)}, u32[]{:S(2)}) %collective-permute-start.8) | collective-permute-done | bytes 163872 | tf_op jit(solution)/shard_map/ppermute | solution.py:28
  25.8 1.8 %collective-permute-start.12 = (bf16[2,32,1280]{2,1,0:T(8,128)(2,1)S(1)}, bf16[2,32,1280]{2,1,0:T(8,128)(2,1)S(1)}, u32[]{:S(2)}, u32[]{:S(2)}) collective-permute-start(bf16[2,32,1280]{2,1,0:T(8,128)(2,1)S(1)} %get-tuple-element.54), channel_id=1, source_target_pairs={{8,0},{12,4},{0,8},{4,12},{9,1},{13,5},{1,9},{5,13},{10,2},{14,6},... | collective-permute-start | bytes 491528 | tf_op jit(solution)/shard_map/ppermute | solution.py:28
  27.8 2.2 %project.5.refs_0_ = f32[64,1280]{1,0:T(8,128)S(1)} custom-call(bf16[32,1280]{1,0:T(8,128)(2,1)S(1)} %activate.5.own_ref, bf16[32,1280]{1,0:T(8,128)(2,1)S(1)} %collective-permute-done.9.got_ref, bf16[6400,1280]{1,0:T(8,128)(2,1)} %down_ref.11), custom_call_target="tpu_custom_call" | custom-call | flops 1 | bytes 1 | tf_op jit(solution)/shard_map/project/pallas_call | solution.py:239
  31.5 2.2 %project.6.refs_0_ = f32[64,1280]{1,0:T(8,128)S(1)} custom-call(bf16[32,1280]{1,0:T(8,128)(2,1)S(1)} %activate.6.own_ref, bf16[32,1280]{1,0:T(8,128)(2,1)S(1)} %collective-permute-done.11.got_ref, bf16[6400,1280]{1,0:T(8,128)(2,1)} %down_ref.11, f32[64,1280]{1,0:T(8,128)S(1)} %project.5.refs_0_), custom_call_target="tpu_custom_call" | custom-call | flops 1 | bytes 1 | tf_op jit(solution)/shard_map/project/pallas_call | solution.py:239
  34.2 1.0 %collective-permute-start.16 = (bf16[2,32,1280]{2,1,0:T(8,128)(2,1)S(1)}, bf16[2,32,1280]{2,1,0:T(8,128)(2,1)S(1)}, u32[]{:S(2)}, u32[]{:S(2)}) collective-permute-start(bf16[2,32,1280]{2,1,0:T(8,128)(2,1)S(1)} %get-tuple-element.60), channel_id=1, source_target_pairs={{8,0},{12,4},{0,8},{4,12},{9,1},{13,5},{1,9},{5,13},{10,2},{14,6},... | collective-permute-start | bytes 491528 | tf_op jit(solution)/shard_map/ppermute | solution.py:28
  35.2 2.2 %project.7.refs_0_ = f32[64,1280]{1,0:T(8,128)S(1)} custom-call(bf16[32,1280]{1,0:T(8,128)(2,1)S(1)} %activate.7.own_ref, bf16[32,1280]{1,0:T(8,128)(2,1)S(1)} %collective-permute-done.13.got_ref, bf16[6400,1280]{1,0:T(8,128)(2,1)} %down_ref.11, f32[64,1280]{1,0:T(8,128)S(1)} %project.6.refs_0_), custom_call_target="tpu_custom_call" | custom-call | flops 1 | bytes 1 | tf_op jit(solution)/shard_map/project/pallas_call | solution.py:239
  37.8 1.0 %collective-permute-done.15.got_ref = bf16[32,1280]{1,0:T(8,128)(2,1)S(1)} collective-permute-done((bf16[32,1280]{1,0:T(8,128)(2,1)S(1)}, bf16[32,1280]{1,0:T(8,128)(2,1)S(1)}, u32[]{:S(2)}, u32[]{:S(2)}) %collective-permute-start.15) | collective-permute-done | bytes 81952 | tf_op jit(solution)/shard_map/ppermute | solution.py:23
  38.8 2.2 %project.8.refs_0_ = f32[64,1280]{1,0:T(8,128)S(1)} custom-call(bf16[32,1280]{1,0:T(8,128)(2,1)S(1)} %activate.8.own_ref, bf16[32,1280]{1,0:T(8,128)(2,1)S(1)} %collective-permute-done.15.got_ref, bf16[6400,1280]{1,0:T(8,128)(2,1)} %down_ref.11, f32[64,1280]{1,0:T(8,128)S(1)} %project.7.refs_0_), custom_call_target="tpu_custom_call" | custom-call | flops 1 | bytes 1 | tf_op jit(solution)/shard_map/project/pallas_call | solution.py:239
  41.5 1.0 %collective-permute-done.17.got_ref = bf16[32,1280]{1,0:T(8,128)(2,1)S(1)} collective-permute-done((bf16[32,1280]{1,0:T(8,128)(2,1)S(1)}, bf16[32,1280]{1,0:T(8,128)(2,1)S(1)}, u32[]{:S(2)}, u32[]{:S(2)}) %collective-permute-start.17) | collective-permute-done | bytes 81952 | tf_op jit(solution)/shard_map/ppermute | solution.py:23
  42.5 2.2 %project.9 = f32[64,1280]{1,0:T(8,128)S(1)} custom-call(bf16[32,1280]{1,0:T(8,128)(2,1)S(1)} %activate.9.own_ref, bf16[32,1280]{1,0:T(8,128)(2,1)S(1)} %collective-permute-done.17.got_ref, bf16[6400,1280]{1,0:T(8,128)(2,1)} %down_ref.11, f32[64,1280]{1,0:T(8,128)S(1)} %project.8.refs_0_), custom_call_target="tpu_custom_call" | custom-call | flops 1 | bytes 1 | tf_op jit(solution)/shard_map/project/pallas_call | solution.py:239
  44.8 1.6 %collective-permute-start.18 = (bf16[16,1280]{1,0:T(8,128)(2,1)S(1)}, bf16[16,1280]{1,0:T(8,128)(2,1)S(1)}, u32[]{:S(2)}, u32[]{:S(2)}) collective-permute-start(bf16[16,1280]{1,0:T(8,128)(2,1)S(1)} %get-tuple-element.63), channel_id=1, source_target_pairs={{0,1},{1,2},{2,3},{3,0},{4,5},{5,6},{6,7},{7,4},{8,9},{9,10},{10,1... | collective-permute-start | bytes 122888 | tf_op jit(solution)/shard_map/ppermute | solution.py:303
  46.4 2.6 %collective-permute-start.19 = (bf16[16,1280]{1,0:T(8,128)(2,1)S(1)}, bf16[16,1280]{1,0:T(8,128)(2,1)S(1)}, u32[]{:S(2)}, u32[]{:S(2)}) collective-permute-start(bf16[16,1280]{1,0:T(8,128)(2,1)S(1)} %get-tuple-element.65), channel_id=1, source_target_pairs={{0,2},{1,3},{2,0},{3,1},{4,6},{5,7},{6,4},{7,5},{8,10},{9,11},{10,... | collective-permute-start | bytes 122888 | tf_op jit(solution)/shard_map/ppermute | solution.py:303
  49.0 1.3 %collective-permute-start.20 = (bf16[16,1280]{1,0:T(8,128)(2,1)S(1)}, bf16[16,1280]{1,0:T(8,128)(2,1)S(1)}, u32[]{:S(2)}, u32[]{:S(2)}) collective-permute-start(bf16[16,1280]{1,0:T(8,128)(2,1)S(1)} %get-tuple-element.64), channel_id=1, source_target_pairs={{0,3},{1,0},{2,1},{3,2},{4,7},{5,4},{6,5},{7,6},{8,11},{9,8},{10,9... | collective-permute-start | bytes 122888 | tf_op jit(solution)/shard_map/ppermute | solution.py:303
  50.6 2.0 %collective-permute-done.19 = bf16[16,1280]{1,0:T(8,128)(2,1)S(1)} collective-permute-done((bf16[16,1280]{1,0:T(8,128)(2,1)S(1)}, bf16[16,1280]{1,0:T(8,128)(2,1)S(1)}, u32[]{:S(2)}, u32[]{:S(2)}) %collective-permute-start.19) | collective-permute-done | bytes 40992 | tf_op jit(solution)/shard_map/ppermute | solution.py:303
  53.0 3.2 %collective-permute-start.21 = (bf16[16,1280]{1,0:T(8,128)(2,1)S(1)}, bf16[16,1280]{1,0:T(8,128)(2,1)S(1)}, u32[]{:S(2)}, u32[]{:S(2)}) collective-permute-start(bf16[16,1280]{1,0:T(8,128)(2,1)S(1)} %fusion.9), channel_id=1, source_target_pairs={{1,0},{2,1},{3,2},{0,3},{5,4},{6,5},{7,6},{4,7},{9,8},{10,9},{11,1... | collective-permute-start | bytes 122888 | tf_op jit(solution)/shard_map/ppermute | solution.py:308
  56.8 1.0 %collective-permute-done.21 = bf16[16,1280]{1,0:T(8,128)(2,1)S(1)} collective-permute-done((bf16[16,1280]{1,0:T(8,128)(2,1)S(1)}, bf16[16,1280]{1,0:T(8,128)(2,1)S(1)}, u32[]{:S(2)}, u32[]{:S(2)}) %collective-permute-start.21) | collective-permute-done | bytes 40992 | tf_op jit(solution)/shard_map/ppermute | solution.py:308
  57.9 3.2 %collective-permute-done.22 = bf16[16,1280]{1,0:T(8,128)(2,1)S(1)} collective-permute-done((bf16[16,1280]{1,0:T(8,128)(2,1)S(1)}, bf16[16,1280]{1,0:T(8,128)(2,1)S(1)}, u32[]{:S(2)}, u32[]{:S(2)}) %collective-permute-start.22) | collective-permute-done | bytes 40992 | tf_op jit(solution)/shard_map/ppermute | solution.py:308
  61.1 0.9 %collective-permute-done.23 = bf16[16,1280]{1,0:T(8,128)(2,1)S(1)} collective-permute-done((bf16[16,1280]{1,0:T(8,128)(2,1)S(1)}, bf16[16,1280]{1,0:T(8,128)(2,1)S(1)}, u32[]{:S(2)}, u32[]{:S(2)}) %collective-permute-start.23) | collective-permute-done | bytes 40992 | tf_op jit(solution)/shard_map/ppermute | solution.py:308
  62.0 1.0 %convolution_convert_fusion = bf16[64,1280]{1,0:T(8,128)(2,1)} fusion(bf16[16,1280]{1,0:T(8,128)(2,1)S(1)} %collective-permute-done.23, bf16[16,1280]{1,0:T(8,128)(2,1)S(1)} %collective-permute-done.22, bf16[16,1280]{1,0:T(8,128)(2,1)S(1)} %collective-permute-done.21, bf16[16,1280]{1,0:T(8,128)(2,1)S(1)} %fusion.9, s32[64]{0:T(128)S(1)} %get-tuple-element.70, ...), kind=kOutput, calls=%fused_computation | convolution fusion | flops 11968512 | bytes 329096 | tf_op jit(solution)/shard_map/dot_general | solution.py:19
  (59 shorter events, 7.5 us)
Async XLA Ops:
  0.0 15.4 %collective-permute-start = (bf16[64,1280]{1,0:T(8,128)(2,1)}, bf16[64,1280]{1,0:T(8,128)(2,1)S(1)}, u32[]{:S(2)}, u32[]{:S(2)}) collective-permute-start(bf16[64,1280]{1,0:T(8,128)(2,1)} %refs_0_.1), channel_id=1, source_target_pairs={{0,4},{4,0},{8,12},{12,8},{1,5},{5,1},{9,13},{13,9},{2,6},{6,2},{1... | collective-permute-start | bytes 491528 | tf_op jit(solution)/shard_map/ppermute | solution.py:23
  0.5 15.0 %collective-permute-start.1 = (bf16[64,1280]{1,0:T(8,128)(2,1)}, bf16[64,1280]{1,0:T(8,128)(2,1)S(1)}, u32[]{:S(2)}, u32[]{:S(2)}) collective-permute-start(bf16[64,1280]{1,0:T(8,128)(2,1)} %refs_0_.1), channel_id=1, source_target_pairs={{8,0},{12,4},{0,8},{4,12},{9,1},{13,5},{1,9},{5,13},{10,2},{14,6},... | collective-permute-start | bytes 491528 | tf_op jit(solution)/shard_map/ppermute | solution.py:28
  3.0 12.4 %collective-permute-start.2 = (bf16[64,1280]{1,0:T(8,128)(2,1)}, bf16[64,1280]{1,0:T(8,128)(2,1)S(1)}, u32[]{:S(2)}, u32[]{:S(2)}) collective-permute-start(bf16[64,1280]{1,0:T(8,128)(2,1)} %refs_0_.1), channel_id=1, source_target_pairs={{12,0},{8,4},{4,8},{0,12},{13,1},{9,5},{5,9},{1,13},{14,2},{10,6},... | collective-permute-start | bytes 491528 | tf_op jit(solution)/shard_map/ppermute | solution.py:28
  17.0 1.5 %collective-permute-start.7 = (bf16[2,32,1280]{2,1,0:T(8,128)(2,1)S(1)}, bf16[2,32,1280]{2,1,0:T(8,128)(2,1)S(1)}, u32[]{:S(2)}, u32[]{:S(2)}) collective-permute-start(bf16[2,32,1280]{2,1,0:T(8,128)(2,1)S(1)} %get-tuple-element.48), channel_id=1, source_target_pairs={{0,4},{4,0},{8,12},{12,8},{1,5},{5,1},{9,13},{13,9},{2,6},{6,2},{1... | collective-permute-start | bytes 491528 | tf_op jit(solution)/shard_map/ppermute | solution.py:23
  17.7 2.6 %collective-permute-start.6 = (bf16[2,32,1280]{2,1,0:T(8,128)(2,1)S(1)}, bf16[2,32,1280]{2,1,0:T(8,128)(2,1)S(1)}, u32[]{:S(2)}, u32[]{:S(2)}) collective-permute-start(bf16[2,32,1280]{2,1,0:T(8,128)(2,1)S(1)} %get-tuple-element.45), channel_id=1, source_target_pairs={{0,4},{4,0},{8,12},{12,8},{1,5},{5,1},{9,13},{13,9},{2,6},{6,2},{1... | collective-permute-start | bytes 491528 | tf_op jit(solution)/shard_map/ppermute | solution.py:23
  18.5 7.1 %collective-permute-start.8 = (bf16[2,32,1280]{2,1,0:T(8,128)(2,1)S(1)}, bf16[2,32,1280]{2,1,0:T(8,128)(2,1)S(1)}, u32[]{:S(2)}, u32[]{:S(2)}) collective-permute-start(bf16[2,32,1280]{2,1,0:T(8,128)(2,1)S(1)} %get-tuple-element.50), channel_id=1, source_target_pairs={{8,0},{12,4},{0,8},{4,12},{9,1},{13,5},{1,9},{5,13},{10,2},{14,6},... | collective-permute-start | bytes 491528 | tf_op jit(solution)/shard_map/ppermute | solution.py:28
  20.3 5.4 %collective-permute-start.5 = (bf16[2,32,1280]{2,1,0:T(8,128)(2,1)S(1)}, bf16[2,32,1280]{2,1,0:T(8,128)(2,1)S(1)}, u32[]{:S(2)}, u32[]{:S(2)}) collective-permute-start(bf16[2,32,1280]{2,1,0:T(8,128)(2,1)S(1)} %get-tuple-element.42), channel_id=1, source_target_pairs={{0,4},{4,0},{8,12},{12,8},{1,5},{5,1},{9,13},{13,9},{2,6},{6,2},{1... | collective-permute-start | bytes 491528 | tf_op jit(solution)/shard_map/ppermute | solution.py:23
  20.4 9.6 %collective-permute-start.10 = (bf16[2,32,1280]{2,1,0:T(8,128)(2,1)S(1)}, bf16[2,32,1280]{2,1,0:T(8,128)(2,1)S(1)}, u32[]{:S(2)}, u32[]{:S(2)}) collective-permute-start(bf16[2,32,1280]{2,1,0:T(8,128)(2,1)S(1)} %get-tuple-element.51), channel_id=1, source_target_pairs={{8,0},{12,4},{0,8},{4,12},{9,1},{13,5},{1,9},{5,13},{10,2},{14,6},... | collective-permute-start | bytes 491528 | tf_op jit(solution)/shard_map/ppermute | solution.py:28
  21.2 9.3 %collective-permute-start.4 = (bf16[2,32,1280]{2,1,0:T(8,128)(2,1)S(1)}, bf16[2,32,1280]{2,1,0:T(8,128)(2,1)S(1)}, u32[]{:S(2)}, u32[]{:S(2)}) collective-permute-start(bf16[2,32,1280]{2,1,0:T(8,128)(2,1)S(1)} %get-tuple-element.39), channel_id=1, source_target_pairs={{0,4},{4,0},{8,12},{12,8},{1,5},{5,1},{9,13},{13,9},{2,6},{6,2},{1... | collective-permute-start | bytes 491528 | tf_op jit(solution)/shard_map/ppermute | solution.py:23
  25.6 2.1 %collective-permute-start.9 = (bf16[32,1280]{1,0:T(8,128)(2,1)S(1)}, bf16[32,1280]{1,0:T(8,128)(2,1)S(1)}, u32[]{:S(2)}, u32[]{:S(2)}) collective-permute-start(bf16[32,1280]{1,0:T(8,128)(2,1)S(1)} %activate.5.own_ref), channel_id=1, source_target_pairs={{0,4},{4,0},{8,12},{12,8},{1,5},{5,1},{9,13},{13,9},{2,6},{6,2},{1... | collective-permute-start | bytes 245768 | tf_op jit(solution)/shard_map/ppermute | solution.py:23
  25.8 7.9 %collective-permute-start.12 = (bf16[2,32,1280]{2,1,0:T(8,128)(2,1)S(1)}, bf16[2,32,1280]{2,1,0:T(8,128)(2,1)S(1)}, u32[]{:S(2)}, u32[]{:S(2)}) collective-permute-start(bf16[2,32,1280]{2,1,0:T(8,128)(2,1)S(1)} %get-tuple-element.54), channel_id=1, source_target_pairs={{8,0},{12,4},{0,8},{4,12},{9,1},{13,5},{1,9},{5,13},{10,2},{14,6},... | collective-permute-start | bytes 491528 | tf_op jit(solution)/shard_map/ppermute | solution.py:28
  27.6 6.6 %collective-permute-start.3 = (bf16[2,32,1280]{2,1,0:T(8,128)(2,1)S(1)}, bf16[2,32,1280]{2,1,0:T(8,128)(2,1)S(1)}, u32[]{:S(2)}, u32[]{:S(2)}) collective-permute-start(bf16[2,32,1280]{2,1,0:T(8,128)(2,1)S(1)} %get-tuple-element.36), channel_id=1, source_target_pairs={{0,4},{4,0},{8,12},{12,8},{1,5},{5,1},{9,13},{13,9},{2,6},{6,2},{1... | collective-permute-start | bytes 491528 | tf_op jit(solution)/shard_map/ppermute | solution.py:23
  30.1 1.3 %collective-permute-start.11 = (bf16[32,1280]{1,0:T(8,128)(2,1)S(1)}, bf16[32,1280]{1,0:T(8,128)(2,1)S(1)}, u32[]{:S(2)}, u32[]{:S(2)}) collective-permute-start(bf16[32,1280]{1,0:T(8,128)(2,1)S(1)} %activate.6.own_ref), channel_id=1, source_target_pairs={{0,4},{4,0},{8,12},{12,8},{1,5},{5,1},{9,13},{13,9},{2,6},{6,2},{1... | collective-permute-start | bytes 245768 | tf_op jit(solution)/shard_map/ppermute | solution.py:23
  30.5 6.9 %collective-permute-start.14 = (bf16[2,32,1280]{2,1,0:T(8,128)(2,1)S(1)}, bf16[2,32,1280]{2,1,0:T(8,128)(2,1)S(1)}, u32[]{:S(2)}, u32[]{:S(2)}) collective-permute-start(bf16[2,32,1280]{2,1,0:T(8,128)(2,1)S(1)} %get-tuple-element.57), channel_id=1, source_target_pairs={{8,0},{12,4},{0,8},{4,12},{9,1},{13,5},{1,9},{5,13},{10,2},{14,6},... | collective-permute-start | bytes 491528 | tf_op jit(solution)/shard_map/ppermute | solution.py:28
  33.8 1.4 %collective-permute-start.13 = (bf16[32,1280]{1,0:T(8,128)(2,1)S(1)}, bf16[32,1280]{1,0:T(8,128)(2,1)S(1)}, u32[]{:S(2)}, u32[]{:S(2)}) collective-permute-start(bf16[32,1280]{1,0:T(8,128)(2,1)S(1)} %activate.7.own_ref), channel_id=1, source_target_pairs={{0,4},{4,0},{8,12},{12,8},{1,5},{5,1},{9,13},{13,9},{2,6},{6,2},{1... | collective-permute-start | bytes 245768 | tf_op jit(solution)/shard_map/ppermute | solution.py:23
  34.2 6.9 %collective-permute-start.16 = (bf16[2,32,1280]{2,1,0:T(8,128)(2,1)S(1)}, bf16[2,32,1280]{2,1,0:T(8,128)(2,1)S(1)}, u32[]{:S(2)}, u32[]{:S(2)}) collective-permute-start(bf16[2,32,1280]{2,1,0:T(8,128)(2,1)S(1)} %get-tuple-element.60), channel_id=1, source_target_pairs={{8,0},{12,4},{0,8},{4,12},{9,1},{13,5},{1,9},{5,13},{10,2},{14,6},... | collective-permute-start | bytes 491528 | tf_op jit(solution)/shard_map/ppermute | solution.py:28
  37.5 1.3 %collective-permute-start.15 = (bf16[32,1280]{1,0:T(8,128)(2,1)S(1)}, bf16[32,1280]{1,0:T(8,128)(2,1)S(1)}, u32[]{:S(2)}, u32[]{:S(2)}) collective-permute-start(bf16[32,1280]{1,0:T(8,128)(2,1)S(1)} %activate.8.own_ref), channel_id=1, source_target_pairs={{0,4},{4,0},{8,12},{12,8},{1,5},{5,1},{9,13},{13,9},{2,6},{6,2},{1... | collective-permute-start | bytes 245768 | tf_op jit(solution)/shard_map/ppermute | solution.py:23
  41.2 1.3 %collective-permute-start.17 = (bf16[32,1280]{1,0:T(8,128)(2,1)S(1)}, bf16[32,1280]{1,0:T(8,128)(2,1)S(1)}, u32[]{:S(2)}, u32[]{:S(2)}) collective-permute-start(bf16[32,1280]{1,0:T(8,128)(2,1)S(1)} %activate.9.own_ref), channel_id=1, source_target_pairs={{0,4},{4,0},{8,12},{12,8},{1,5},{5,1},{9,13},{13,9},{2,6},{6,2},{1... | collective-permute-start | bytes 245768 | tf_op jit(solution)/shard_map/ppermute | solution.py:23
  44.8 5.9 %collective-permute-start.18 = (bf16[16,1280]{1,0:T(8,128)(2,1)S(1)}, bf16[16,1280]{1,0:T(8,128)(2,1)S(1)}, u32[]{:S(2)}, u32[]{:S(2)}) collective-permute-start(bf16[16,1280]{1,0:T(8,128)(2,1)S(1)} %get-tuple-element.63), channel_id=1, source_target_pairs={{0,1},{1,2},{2,3},{3,0},{4,5},{5,6},{6,7},{7,4},{8,9},{9,10},{10,1... | collective-permute-start | bytes 122888 | tf_op jit(solution)/shard_map/ppermute | solution.py:303
  46.4 6.2 %collective-permute-start.19 = (bf16[16,1280]{1,0:T(8,128)(2,1)S(1)}, bf16[16,1280]{1,0:T(8,128)(2,1)S(1)}, u32[]{:S(2)}, u32[]{:S(2)}) collective-permute-start(bf16[16,1280]{1,0:T(8,128)(2,1)S(1)} %get-tuple-element.65), channel_id=1, source_target_pairs={{0,2},{1,3},{2,0},{3,1},{4,6},{5,7},{6,4},{7,5},{8,10},{9,11},{10,... | collective-permute-start | bytes 122888 | tf_op jit(solution)/shard_map/ppermute | solution.py:303
  49.0 4.0 %collective-permute-start.20 = (bf16[16,1280]{1,0:T(8,128)(2,1)S(1)}, bf16[16,1280]{1,0:T(8,128)(2,1)S(1)}, u32[]{:S(2)}, u32[]{:S(2)}) collective-permute-start(bf16[16,1280]{1,0:T(8,128)(2,1)S(1)} %get-tuple-element.64), channel_id=1, source_target_pairs={{0,3},{1,0},{2,1},{3,2},{4,7},{5,4},{6,5},{7,6},{8,11},{9,8},{10,9... | collective-permute-start | bytes 122888 | tf_op jit(solution)/shard_map/ppermute | solution.py:303
  53.0 4.9 %collective-permute-start.21 = (bf16[16,1280]{1,0:T(8,128)(2,1)S(1)}, bf16[16,1280]{1,0:T(8,128)(2,1)S(1)}, u32[]{:S(2)}, u32[]{:S(2)}) collective-permute-start(bf16[16,1280]{1,0:T(8,128)(2,1)S(1)} %fusion.9), channel_id=1, source_target_pairs={{1,0},{2,1},{3,2},{0,3},{5,4},{6,5},{7,6},{4,7},{9,8},{10,9},{11,1... | collective-permute-start | bytes 122888 | tf_op jit(solution)/shard_map/ppermute | solution.py:308
  56.2 4.9 %collective-permute-start.22 = (bf16[16,1280]{1,0:T(8,128)(2,1)S(1)}, bf16[16,1280]{1,0:T(8,128)(2,1)S(1)}, u32[]{:S(2)}, u32[]{:S(2)}) collective-permute-start(bf16[16,1280]{1,0:T(8,128)(2,1)S(1)} %fusion.9), channel_id=1, source_target_pairs={{2,0},{3,1},{0,2},{1,3},{6,4},{7,5},{4,6},{5,7},{10,8},{11,9},{8,1... | collective-permute-start | bytes 122888 | tf_op jit(solution)/shard_map/ppermute | solution.py:308
  56.2 5.8 %collective-permute-start.23 = (bf16[16,1280]{1,0:T(8,128)(2,1)S(1)}, bf16[16,1280]{1,0:T(8,128)(2,1)S(1)}, u32[]{:S(2)}, u32[]{:S(2)}) collective-permute-start(bf16[16,1280]{1,0:T(8,128)(2,1)S(1)} %fusion.9), channel_id=1, source_target_pairs={{3,0},{0,1},{1,2},{2,3},{7,4},{4,5},{5,6},{6,7},{11,8},{8,9},{9,10... | collective-permute-start | bytes 122888 | tf_op jit(solution)/shard_map/ppermute | solution.py:308
  (5 other events, 54.7 us)

commit v3 on v2

v3 whole, which is shorter than its diff:
```python
import functools

import jax
import jax.numpy as jnp
from jax import lax
from jax.experimental import pallas as pl
from jax.experimental.pallas import tpu as pltpu
from jax.sharding import PartitionSpec as P

low_rank_scale = 0.5
f32 = jnp.float32
bf16 = jnp.bfloat16
MIB = 1 << 20
CHUNKS = (2560, 2560, 1280)
PIECE = 256


def dot(a, b):
    return jnp.dot(a, b, preferred_element_type=f32)


def core_swap(value, replicas):
    return lax.ppermute(value, "replica", [(i, i ^ 1) for i in range(replicas)])


def from_chip(value, replicas, step, flip=0):
    pairs = [((i + 2 * step) % replicas ^ flip, i) for i in range(replicas)]
    return lax.ppermute(value, "replica", pairs)


def row_order(rows, block, chips, me):
    mine = lax.broadcasted_iota(jnp.int32, (rows, rows), 0)
    batch = lax.broadcasted_iota(jnp.int32, (rows, rows), 1)
    nth = mine // block
    chip = (me // 2 + nth % chips) % chips
    core = (me % 2 + nth // chips) % 2
    return (batch == (chip * 2 + core) * block + mine % block).astype(f32).astype(bf16)


def widen_into(spread, expand_ref, base_ref, at, start, own_ref, away_ref):
    _, half, width = own_ref.shape
    rows = 2 * half
    delta = dot(spread, expand_ref[:, start : start + width])
    delta = (low_rank_scale * delta).astype(bf16).astype(f32)
    for p in range(2):
        total = base_ref[p, :, at : at + width] + delta[p * rows : (p + 1) * rows]
        own_ref[p] = total[:half]
        away_ref[p] = total[half:].astype(bf16)


def shrink_kernel(block, sources, ids_ref, slots_ref, down_ref, expand_ref, base_ref, *refs):
    pieces, (spread_ref, own_ref, away_ref) = refs[:-3], refs[-3:]
    me = lax.axis_index("replica")
    rows, width = pieces[0].shape
    stored, _, rank, _ = down_ref.shape
    table = stored * 2 * rank
    total = jnp.zeros((rows, table), f32)
    for piece, source in zip(pieces, sources(me)):
        columns = pl.ds(pl.multiple_of(source * width, 128), width)
        part = down_ref[:, :, :, columns].reshape(table, width)
        total += lax.dot_general(piece[...], part, (((1,), (1,)), ((), ())), preferred_element_type=f32)
    shrink = total.astype(bf16).astype(f32)
    adapters = slots_ref.shape[1]
    known = lax.broadcasted_iota(jnp.int32, (adapters, rows), 0)
    chosen = (known == ids_ref[...]).astype(f32).astype(bf16)
    slots = jnp.broadcast_to(slots_ref[...].astype(f32), (table, adapters)).astype(bf16)
    slot = lax.dot_general(chosen, slots, (((0,), (1,)), ((), ())), preferred_element_type=f32)
    first = (slot.astype(jnp.int32) - me * stored) * (2 * rank)
    column = lax.broadcasted_iota(jnp.int32, (rows, table), 1)
    order = row_order(rows, block, len(pieces) // 2, me)
    for p in range(2):
        begin = first + p * rank
        mine = jnp.logical_and(column >= begin, column < begin + rank)
        picked = jnp.where(mine, shrink, 0.0).astype(bf16)
        spread_ref[p * rows : (p + 1) * rows] = dot(order, picked).astype(bf16)
    widen_into(spread_ref[...], expand_ref, base_ref, 0, 0, own_ref, away_ref)


def parted(half, width):
    return [jax.ShapeDtypeStruct((2, half, width), f32), jax.ShapeDtypeStruct((2, half, width), bf16)]


def shrink_rows(pieces, sources, block, ids, slots, adapter_down, expand, base, width):
    rows = ids.shape[0]
    vmem = pl.BlockSpec(memory_space=pltpu.VMEM)
    return pl.pallas_call(
        functools.partial(shrink_kernel, block, sources),
        out_shape=[jax.ShapeDtypeStruct((2 * rows, expand.shape[0]), bf16)] + parted(rows // 2, width),
        in_specs=[vmem] * (5 + len(pieces)),
        out_specs=[vmem] * 3,
        compiler_params=pltpu.CompilerParams(vmem_limit_bytes=(16 if rows <= 64 else 40) * MIB),
        cost_estimate=pl.CostEstimate(
            flops=2 * adapter_down.size * rows, bytes_accessed=2 * adapter_down.size, transcendentals=0
        ),
        name="shrink",
    )(ids.reshape(1, rows), slots.reshape(1, -1), adapter_down, expand, base, *pieces)


def widen_kernel(widths, at, start, spread_ref, expand_ref, base_ref, *out_refs):
    for k, width in enumerate(widths):
        widen_into(spread_ref[...], expand_ref, base_ref, at, start, out_refs[2 * k], out_refs[2 * k + 1])
        at += width
        start += width


def widen(spread, expand, base, at, start, widths):
    half = spread.shape[0] // 4
    vmem = pl.BlockSpec(memory_space=pltpu.VMEM)
    return pl.pallas_call(
        functools.partial(widen_kernel, widths, at, start),
        out_shape=[shape for width in widths for shape in parted(half, width)],
        in_specs=[vmem] * 3,
        out_specs=[vmem] * (2 * len(widths)),
        compiler_params=pltpu.CompilerParams(vmem_limit_bytes=16 * MIB),
        cost_estimate=pl.CostEstimate(
            flops=2 * spread.size * sum(widths), bytes_accessed=4 * spread.size, transcendentals=0
        ),
        name="widen",
    )(spread, expand, base)


def stream_kernel(block, chips, start, tile, x_ref, gate_ref, up_ref, out_ref, rows_in, mixed, held, arrived):
    slots = held.shape[0]
    rows = x_ref.shape[0]
    work = [(p, at) for at in range(0, out_ref.shape[2], tile) for p in range(2)]

    def fetch(i):
        p, at = work[i]
        source = (gate_ref, up_ref)[p].at[:, pl.ds(start + at, tile)]
        return pltpu.make_async_copy(source, held.at[i % slots], arrived.at[i % slots])

    enter = pltpu.make_async_copy(x_ref, rows_in, arrived.at[slots])
    enter.start()
    for i in range(min(slots, len(work))):
        fetch(i).start()
    order = row_order(rows, block, chips, lax.axis_index("replica"))
    enter.wait()
    mixed[...] = dot(order, rows_in[...]).astype(bf16)
    for i, (p, at) in enumerate(work):
        fetch(i).wait()
        out_ref[p, :, at : at + tile] = dot(mixed[...], held[i % slots])
        if i + slots < len(work):
            fetch(i + slots).start()


def stream(x, gate, up, block, chips, start, width, slots=8):
    rows, depth = x.shape
    tile = max(t for t in range(128, 641, 128) if width % t == 0)
    far = pl.BlockSpec(memory_space=pltpu.HBM)
    return pl.pallas_call(
        functools.partial(stream_kernel, block, chips, start, tile),
        out_shape=jax.ShapeDtypeStruct((2, rows, width), f32),
        in_specs=[far] * 3,
        out_specs=pl.BlockSpec(memory_space=pltpu.VMEM),
        scratch_shapes=[
            pltpu.VMEM((rows, depth), bf16),
            pltpu.VMEM((rows, depth), bf16),
            pltpu.VMEM((slots, depth, tile), bf16),
            pltpu.SemaphoreType.DMA((slots + 1,)),
        ],
        compiler_params=pltpu.CompilerParams(vmem_limit_bytes=50 * MIB),
        cost_estimate=pl.CostEstimate(
            flops=4 * rows * depth * width, bytes_accessed=4 * depth * width, transcendentals=0
        ),
        name="stream",
    )(x, gate, up)


def join_kernel(own_ref, got_ref, sum_ref, *send_refs):
    block = sum_ref.shape[1]
    total = own_ref[...] + got_ref[...].astype(f32)
    sum_ref[...] = total[:, :block]
    for step, send_ref in enumerate(send_refs, 1):
        send_ref[...] = total[:, step * block : (step + 1) * block].astype(bf16)


def join(block, own, got):
    vmem = pl.BlockSpec(memory_space=pltpu.VMEM)
    _, half, width = own.shape
    away = half // block - 1
    return pl.pallas_call(
        join_kernel,
        out_shape=[jax.ShapeDtypeStruct((2, block, width), f32)]
        + [jax.ShapeDtypeStruct((2, block, width), bf16)] * away,
        in_specs=[vmem] * 2,
        out_specs=[vmem] * (1 + away),
        compiler_params=pltpu.CompilerParams(vmem_limit_bytes=8 * MIB),
        cost_estimate=pl.CostEstimate(flops=1, bytes_accessed=1, transcendentals=0),
        name="join",
    )(own, got)


def activate_kernel(own_ref, *refs):
    def total(p):
        sums = own_ref[p]
        for got_ref in refs[:-1]:
            sums += got_ref[p].astype(f32)
        return sums

    gate, up = total(0), total(1)
    refs[-1][...] = (gate / (1.0 + jnp.exp(-gate)) * up).astype(bf16)


def activate(own, gots):
    vmem = pl.BlockSpec(memory_space=pltpu.VMEM)
    return pl.pallas_call(
        activate_kernel,
        out_shape=jax.ShapeDtypeStruct(own.shape[1:], bf16),
        in_specs=[vmem] * (1 + len(gots)),
        out_specs=vmem,
        compiler_params=pltpu.CompilerParams(vmem_limit_bytes=8 * MIB),
        cost_estimate=pl.CostEstimate(flops=1, bytes_accessed=1, transcendentals=0),
        name="activate",
    )(own, *gots)


def fetch_kernel(down_ref, after_ref, out_ref, arrived):
    copy = pltpu.make_async_copy(down_ref.at[pl.ds(0, out_ref.shape[0])], out_ref, arrived)
    copy.start()
    copy.wait()


def fetch(down, after, rows):
    far = pl.BlockSpec(memory_space=pltpu.HBM)
    return pl.pallas_call(
        fetch_kernel,
        out_shape=jax.ShapeDtypeStruct((rows, down.shape[1]), bf16),
        in_specs=[far, pl.BlockSpec(memory_space=pl.ANY)],
        out_specs=pl.BlockSpec(memory_space=pltpu.VMEM),
        scratch_shapes=[pltpu.SemaphoreType.DMA(())],
        compiler_params=pltpu.CompilerParams(vmem_limit_bytes=40 * MIB),
        cost_estimate=pl.CostEstimate(flops=1, bytes_accessed=1, transcendentals=0),
        name="fetch",
    )(down, after)


def project_kernel(count, near_ref, down_ref, *refs):
    blocks, (total_ref, hidden, held, arrived) = refs[:-4], refs[-4:]
    pieces, depth, columns = held.shape
    near = near_ref.shape[0]

    def bring(i):
        source = down_ref.at[pl.ds(near + i * depth, depth)]
        return pltpu.make_async_copy(source, held.at[i], arrived.at[i])

    for i in range(pieces):
        bring(i).start()
    me = lax.axis_index("replica")
    chips = count // 2
    start = 0
    for c in range(len(blocks) // count):
        parts = blocks[c * count : (c + 1) * count]
        block, width = parts[0].shape
        for nth, ref in enumerate(parts):
            chip = (me // 2 + nth % chips) % chips
            at = (chip * 2 + (me + nth // chips) % 2) * block
            hidden[pl.ds(pl.multiple_of(at, 16), block), start : start + width] = ref[...]
        start += width
    total = dot(hidden[:, :near], near_ref[...])
    for i in range(pieces):
        bring(i).wait()
        total += dot(hidden[:, near + i * depth : near + (i + 1) * depth], held[i])
    total_ref[...] = total.astype(bf16)


def project(chunks, near, down):
    count = len(chunks[0])
    rows = count * chunks[0][0].shape[0]
    vmem = pl.BlockSpec(memory_space=pltpu.VMEM)
    far = pl.BlockSpec(memory_space=pltpu.HBM)
    blocks = [value for chunk in chunks for value in chunk]
    pieces = (down.shape[0] - near.shape[0]) // PIECE
    return pl.pallas_call(
        functools.partial(project_kernel, count),
        out_shape=jax.ShapeDtypeStruct((rows, down.shape[1]), bf16),
        in_specs=[vmem, far] + [vmem] * len(blocks),
        out_specs=vmem,
        scratch_shapes=[
            pltpu.VMEM((rows, down.shape[0]), bf16),
            pltpu.VMEM((pieces, PIECE, down.shape[1]), bf16),
            pltpu.SemaphoreType.DMA((pieces,)),
        ],
        compiler_params=pltpu.CompilerParams(vmem_limit_bytes=40 * MIB),
        cost_estimate=pl.CostEstimate(
            flops=2 * rows * down.size, bytes_accessed=2 * down.size, transcendentals=0
        ),
        name="project",
    )(near, down, *blocks)


def shards(
    tokens, gate_matrix, up_matrix, down_weight, adapter_down, adapter_up, adapter_ids, adapter_slot
):
    replicas, depth = lax.axis_size("replica"), lax.axis_size("tensor")
    chips = replicas // 2
    rows = tokens.shape[0]
    block = rows // replicas
    half = rows // 2
    units = gate_matrix.shape[1]

    pieces = [tokens, core_swap(tokens, replicas)]
    for step in range(1, chips):
        for flip in range(2):
            pieces.append(from_chip(tokens, replicas, step, flip))

    def sources(me):
        far = [((me + 2 * step) % replicas, flip) for step in range(1, chips) for flip in range(2)]
        near = [(me, 0), (me, 1)]
        return [at + flip * (1 - 2 * (at % 2)) for at, flip in near + far]

    widths = CHUNKS if sum(CHUNKS) == units else (units,)
    base = stream(tokens, gate_matrix, up_matrix, block, chips, 0, units)
    expand = adapter_up.reshape(-1, units)
    spread, *parts = shrink_rows(
        pieces, sources, block, adapter_ids, adapter_slot, adapter_down, expand, base, widths[0]
    )
    if len(widths) > 1:
        parts += widen(spread, expand, base, widths[0], widths[0], widths[1:])
    sums = []
    for own, away in zip(parts[::2], parts[1::2]):
        own, *sends = join(block, own, core_swap(away, replicas))
        gots = [from_chip(send, replicas, chips - step) for step, send in enumerate(sends, 1)]
        sums.append((own, gots))
    chunks = []
    near = fetch(down_weight, sums[-1][0], units * 3 // 5)
    own, gots = sums[0]
    near, *gots = lax.optimization_barrier((near, *gots))
    sums[0] = own, gots
    for own, gots in sums:
        hidden = activate(own, gots)
        blocks = [hidden] + [from_chip(hidden, replicas, step) for step in range(1, chips)]
        chunks.append(blocks + [core_swap(value, replicas) for value in blocks])
    total = project(chunks, near, down_weight)
    reach = 1
    while reach < depth:
        pairs = [(i, i ^ (2 * reach - 1)) for i in range(depth)]
        total = (total.astype(f32) + lax.ppermute(total, "tensor", pairs).astype(f32)).astype(bf16)
        reach *= 2
    return total


def solution(mesh):
    placed = (
        P("groups", "replica"),
        P("replica", "tensor"),
        P("replica", "tensor"),
        P("tensor", "replica"),
        P("replica", None, None, None),
        P("replica", None, None, "tensor"),
        P("groups"),
        P("groups"),
    )
    return jax.shard_map(
        shards, mesh=mesh, in_specs=placed, out_specs=P("groups", "replica"), check_vma=False
    )
```

time: 63.2 us -> 57.2 us (0.905)
  Pallas kernels: 25 us -> 22.3 us
  starting transfers between devices: 21.1 us -> 19.4 us
  waiting for transfers between devices: 14.6 us -> 13.3 us
  matrix products: 1.04 us -> 0 us
  other arithmetic: 0.05 us -> 0.75 us
    ppermute x6 -> x2, starting transfers between devices: 9.38 us -> 5.48 us  [shards(): lax.ppermute(total, 'tensor', pairs).astype(f32)]
    ppermute x7 -> x8, starting transfers between devices: 8.88 us -> 12 us  [from_chip(): return lax.ppermute(value, 'replica', pairs)]
    pallas_call x17 -> x10, Pallas kernels: 23.6 us -> 20.6 us  [the longest x1 11.5 us: stream(): pl.pallas_call(functools.partial(stream_kernel, block, chips, start, tile...]
    ppermute x7 -> x8, waiting for transfers between devices: 4.36 us -> 2.87 us  [from_chip(): return lax.ppermute(value, 'replica', pairs)]
    dot_general x1 -> x0, matrix products: 1.04 us -> none  [dot(): return jnp.dot(a, b, preferred_element_type=f32)]
    ppermute x11 -> x10, starting transfers between devices: 2.83 us -> 1.9 us  [core_swap(): return lax.ppermute(value, 'replica', [(i, i ^ 1) for i in range(replicas)])]
    convert_element_type x1 -> x2, other arithmetic: 0.02 us -> 0.75 us  [shards(): (total.astype(f32) + lax.ppermute(total, 'tensor', pairs).astype(f32)).as...]
    ppermute x6 -> x2, waiting for transfers between devices: 7.83 us -> 8.42 us  [shards(): lax.ppermute(total, 'tensor', pairs).astype(f32)]
  transfers between devices with their start and end apart: 24 -> 20, of which waited for: 11 -> 7; matrix products, arithmetic and copies ran while one was open for 0% -> 0% of each run, Pallas kernels for 34% -> 28%
where the time goes in v3:
time: 57.2 us; the launch traced here: 56.9 us
  Pallas kernels  22.3 us (39%)
  starting transfers between devices  19.4 us (34%)
  waiting for transfers between devices  13.3 us (23%)
  local copies, waits for them, and re-layouts  0.96 us (2%)
  other arithmetic  0.75 us (1%)
    ppermute x8, starting transfers between devices, from_chip(): return lax.ppermute(value, 'replica', pairs)  12 us
    pallas_call x1, Pallas kernels, stream(): pl.pallas_call(functools.partial(stream_kernel, block, chips, start, tile...  11.5 us
    ppermute x2, waiting for transfers between devices, shards(): lax.ppermute(total, 'tensor', pairs).astype(f32)  8.42 us
    ppermute x2, starting transfers between devices, shards(): lax.ppermute(total, 'tensor', pairs).astype(f32)  5.48 us
    pallas_call x1, Pallas kernels, project(): pl.pallas_call(functools.partial(project_kernel, count), out_shape=jax.Sh...  4.49 us
    pallas_call x1, Pallas kernels, fetch(): pl.pallas_call(fetch_kernel, out_shape=jax.ShapeDtypeStruct((rows, down.s...  3.8 us
    ppermute x8, waiting for transfers between devices, from_chip(): return lax.ppermute(value, 'replica', pairs)  2.87 us
    ppermute x10, waiting for transfers between devices, core_swap(): return lax.ppermute(value, 'replica', [(i, i ^ 1) for i in range(replicas)])  2.04 us
  transfers between devices with their start and end apart: 20, of which 7 were waited for; matrix products, arithmetic and copies ran while one was open for 0% of the time, Pallas kernels for 28%

profile of v3, /device:TPU:0, one launch (start us, length us, event | category | flops | bytes accessed | tf_op | source)
XLA Modules:
  0.0 56.9 jit_solution(12089290912682491969)
XLA Ops:
  0.0 3.0 %collective-permute-start.1 = (bf16[64,1280]{1,0:T(8,128)(2,1)}, bf16[64,1280]{1,0:T(8,128)(2,1)S(1)}, u32[]{:S(2)}, u32[]{:S(2)}) collective-permute-start(bf16[64,1280]{1,0:T(8,128)(2,1)} %refs_0_.1), channel_id=1, source_target_pairs={{8,0},{12,4},{0,8},{4,12},{9,1},{13,5},{1,9},{5,13},{10,2},{14,6},... | collective-permute-start | bytes 491528 | tf_op jit(solution)/shard_map/ppermute | solution.py:28
  3.2 0.9 %copy-done.2 = bf16[64,1280]{1,0:T(8,128)(2,1)S(1)} copy-done((bf16[64,1280]{1,0:T(8,128)(2,1)S(1)}, bf16[64,1280]{1,0:T(8,128)(2,1)}, u32[]{:S(2)}) %copy-start.2) | copy-done | bytes 163864
  4.1 11.5 %stream.1.base_ref = f32[2,64,6400]{2,1,0:T(8,128)S(1)} custom-call(bf16[64,1280]{1,0:T(8,128)(2,1)S(1)} %copy-done.2, bf16[1280,6400]{1,0:T(8,128)(2,1)} %gate_ref.1, bf16[1280,6400]{1,0:T(8,128)(2,1)} %up_ref.1), custom_call_target="tpu_custom_call" | custom-call | flops 2097152000 | bytes 32768000 | tf_op jit(solution)/shard_map/stream/pallas_call | solution.py:150
  15.7 1.7 %shrink.1 = (bf16[128,256]{1,0:T(8,128)(2,1)S(1)}, f32[2,32,2560]{2,1,0:T(8,128)S(1)}, bf16[2,32,2560]{2,1,0:T(8,128)(2,1)S(1)}) custom-call(s32[1,64]{1,0:T(1,128)S(1)} %bitcast.5, s32[1,32]{1,0:T(1,128)S(1)} %bitcast.6, bf16[8,2,16,5120]{3,2,1,0:T(8,128)(2,1)S(1)} %copy-done.1, bf16[256,6400]{1,0:T(8,128)(2,1)S(1)} %bitcast.3, ...), custom_call_target="tpu_custom_call" | custom-call | flops 167772160 | bytes 2621440 | tf_op jit(solution)/shard_map/shrink/pallas_call | solution.py:86
  17.4 0.4 widen.1
  17.9 0.4 collective-permute-start.9
  18.8 0.8 %collective-permute-done.9.got_ref = bf16[2,32,2560]{2,1,0:T(8,128)(2,1)S(1)} collective-permute-done((bf16[2,32,2560]{2,1,0:T(8,128)(2,1)S(1)}, bf16[2,32,2560]{2,1,0:T(8,128)(2,1)S(1)}, u32[]{:S(2)}, u32[]{:S(2)}) %collective-permute-start.9) | collective-permute-done | bytes 327712 | tf_op jit(solution)/shard_map/ppermute | solution.py:23
  19.6 2.0 %collective-permute-start.10 = (bf16[2,16,2560]{2,1,0:T(8,128)(2,1)S(1)}, bf16[2,16,2560]{2,1,0:T(8,128)(2,1)S(1)}, u32[]{:S(2)}, u32[]{:S(2)}) collective-permute-start(bf16[2,16,2560]{2,1,0:T(8,128)(2,1)S(1)} %get-tuple-element.33), channel_id=1, source_target_pairs={{8,0},{12,4},{0,8},{4,12},{9,1},{13,5},{1,9},{5,13},{10,2},{14,6},... | collective-permute-start | bytes 491528 | tf_op jit(solution)/shard_map/ppermute | solution.py:28
  21.7 0.4 collective-permute-start.5
  22.2 1.8 %collective-permute-start.14 = (bf16[2,16,1280]{2,1,0:T(8,128)(2,1)S(1)}, bf16[2,16,1280]{2,1,0:T(8,128)(2,1)S(1)}, u32[]{:S(2)}, u32[]{:S(2)}) collective-permute-start(bf16[2,16,1280]{2,1,0:T(8,128)(2,1)S(1)} %get-tuple-element.34), channel_id=1, source_target_pairs={{8,0},{12,4},{0,8},{4,12},{9,1},{13,5},{1,9},{5,13},{10,2},{14,6},... | collective-permute-start | bytes 245768 | tf_op jit(solution)/shard_map/ppermute | solution.py:28
  23.9 3.8 %fetch.1.near_ref = bf16[3840,1280]{1,0:T(8,128)(2,1)S(1)} custom-call(bf16[6400,1280]{1,0:T(8,128)(2,1)} %down_ref.5, f32[2,16,1280]{2,1,0:T(8,128)S(1)} %get-tuple-element.23.after_ref.own_ref), custom_call_target="tpu_custom_call" | custom-call | flops 1 | bytes 1 | tf_op jit(solution)/shard_map/fetch/pallas_call | solution.py:225
  27.8 1.0 %collective-permute-start.11 = (bf16[16,2560]{1,0:T(8,128)(2,1)S(1)}, bf16[16,2560]{1,0:T(8,128)(2,1)S(1)}, u32[]{:S(2)}, u32[]{:S(2)}) collective-permute-start(bf16[16,2560]{1,0:T(8,128)(2,1)S(1)} %activate.4.refs_4_), channel_id=1, source_target_pairs={{8,0},{12,4},{0,8},{4,12},{9,1},{13,5},{1,9},{5,13},{10,2},{14,6},... | collective-permute-start | bytes 245768 | tf_op jit(solution)/shard_map/ppermute | solution.py:28
  28.8 1.4 %collective-permute-done.5.refs_0_ = bf16[2,16,2560]{2,1,0:T(8,128)(2,1)S(1)} collective-permute-done((bf16[2,16,2560]{2,1,0:T(8,128)(2,1)S(1)}, bf16[2,16,2560]{2,1,0:T(8,128)(2,1)S(1)}, u32[]{:S(2)}, u32[]{:S(2)}) %collective-permute-start.5) | collective-permute-done | bytes 163872 | tf_op jit(solution)/shard_map/ppermute | solution.py:28
  30.3 2.0 %collective-permute-start.6 = (bf16[16,2560]{1,0:T(8,128)(2,1)S(1)}, bf16[16,2560]{1,0:T(8,128)(2,1)S(1)}, u32[]{:S(2)}, u32[]{:S(2)}) collective-permute-start(bf16[16,2560]{1,0:T(8,128)(2,1)S(1)} %activate.3.refs_0_), channel_id=1, source_target_pairs={{8,0},{12,4},{0,8},{4,12},{9,1},{13,5},{1,9},{5,13},{10,2},{14,6},... | collective-permute-start | bytes 245768 | tf_op jit(solution)/shard_map/ppermute | solution.py:28
  32.4 1.7 %collective-permute-start.15 = (bf16[16,1280]{1,0:T(8,128)(2,1)S(1)}, bf16[16,1280]{1,0:T(8,128)(2,1)S(1)}, u32[]{:S(2)}, u32[]{:S(2)}) collective-permute-start(bf16[16,1280]{1,0:T(8,128)(2,1)S(1)} %activate.5.refs_8_), channel_id=1, source_target_pairs={{8,0},{12,4},{0,8},{4,12},{9,1},{13,5},{1,9},{5,13},{10,2},{14,6},... | collective-permute-start | bytes 122888 | tf_op jit(solution)/shard_map/ppermute | solution.py:28
  34.3 0.3 collective-permute-start.7
  35.2 1.4 %collective-permute-done.15.refs_9_ = bf16[16,1280]{1,0:T(8,128)(2,1)S(1)} collective-permute-done((bf16[16,1280]{1,0:T(8,128)(2,1)S(1)}, bf16[16,1280]{1,0:T(8,128)(2,1)S(1)}, u32[]{:S(2)}, u32[]{:S(2)}) %collective-permute-start.15) | collective-permute-done | bytes 40992 | tf_op jit(solution)/shard_map/ppermute | solution.py:28
  36.5 1.2 %collective-permute-done.17.refs_11_ = bf16[16,1280]{1,0:T(8,128)(2,1)S(1)} collective-permute-done((bf16[16,1280]{1,0:T(8,128)(2,1)S(1)}, bf16[16,1280]{1,0:T(8,128)(2,1)S(1)}, u32[]{:S(2)}, u32[]{:S(2)}) %collective-permute-start.17) | collective-permute-done | bytes 40992 | tf_op jit(solution)/shard_map/ppermute | solution.py:23
  37.8 4.5 %project.1 = bf16[64,1280]{1,0:T(8,128)(2,1)S(1)} custom-call(bf16[3840,1280]{1,0:T(8,128)(2,1)S(1)} %fetch.1.near_ref, bf16[6400,1280]{1,0:T(8,128)(2,1)} %down_ref.5, bf16[16,2560]{1,0:T(8,128)(2,1)S(1)} %activate.3.refs_0_, bf16[16,2560]{1,0:T(8,128)(2,1)S(1)} %collective-permute-done.6.refs_1_, bf16[16,2560]{1,0:T(8,128)(2,1)S(1)} %collective-permute-done.7.refs_2_, ...), custom_call_target="tpu_custom_call" | custom-call | flops 1048576000 | bytes 16384000 | tf_op jit(solution)/shard_map/project/pallas_call | solution.py:273
  42.3 1.7 %collective-permute-start.18 = (bf16[64,1280]{1,0:T(8,128)(2,1)S(1)}, bf16[64,1280]{1,0:T(8,128)(2,1)S(1)}, u32[]{:S(2)}, u32[]{:S(2)}) collective-permute-start(bf16[64,1280]{1,0:T(8,128)(2,1)S(1)} %project.1), channel_id=1, source_target_pairs={{0,1},{1,0},{2,3},{3,2},{4,5},{5,4},{6,7},{7,6},{8,9},{9,8},{10,11... | collective-permute-start | bytes 491528 | tf_op jit(solution)/shard_map/ppermute | solution.py:337
  44.0 4.6 %collective-permute-done.18 = bf16[64,1280]{1,0:T(8,128)(2,1)S(1)} collective-permute-done((bf16[64,1280]{1,0:T(8,128)(2,1)S(1)}, bf16[64,1280]{1,0:T(8,128)(2,1)S(1)}, u32[]{:S(2)}, u32[]{:S(2)}) %collective-permute-start.18) | collective-permute-done | bytes 163872 | tf_op jit(solution)/shard_map/ppermute | solution.py:337
  48.6 3.8 %collective-permute-start.19 = (bf16[64,1280]{1,0:T(8,128)(2,1)S(1)}, bf16[64,1280]{1,0:T(8,128)(2,1)S(1)}, u32[]{:S(2)}, u32[]{:S(2)}) collective-permute-start(bf16[64,1280]{1,0:T(8,128)(2,1)S(1)} %add_convert_fusion.1), channel_id=1, source_target_pairs={{0,3},{1,2},{2,1},{3,0},{4,7},{5,6},{6,5},{7,4},{8,11},{9,10},{10,... | collective-permute-start | bytes 491528 | tf_op jit(solution)/shard_map/ppermute | solution.py:337
  52.4 3.8 %collective-permute-done.19 = bf16[64,1280]{1,0:T(8,128)(2,1)S(1)} collective-permute-done((bf16[64,1280]{1,0:T(8,128)(2,1)S(1)}, bf16[64,1280]{1,0:T(8,128)(2,1)S(1)}, u32[]{:S(2)}, u32[]{:S(2)}) %collective-permute-start.19) | collective-permute-done | bytes 163872 | tf_op jit(solution)/shard_map/ppermute | solution.py:337
  56.2 0.7 %add_convert_fusion = bf16[64,1280]{1,0:T(8,128)(2,1)} fusion(bf16[64,1280]{1,0:T(8,128)(2,1)S(1)} %collective-permute-done.19, bf16[64,1280]{1,0:T(8,128)(2,1)S(1)} %add_convert_fusion.1), kind=kLoop, calls=%fused_computation | loop fusion | flops 327680 | bytes 491520 | tf_op jit(solution)/shard_map/convert_element_type | solution.py:337
  (39 shorter events, 1.9 us)
Async XLA Ops:
  0.0 15.7 %copy-start = (bf16[8,2,16,6400]{3,2,1,0:T(8,128)(2,1)S(1)}, bf16[8,2,16,6400]{3,2,1,0:T(8,128)(2,1)}, u32[]{:S(2)}) copy-start(bf16[8,2,16,6400]{3,2,1,0:T(8,128)(2,1)} %param.13) | copy-start | bytes 9830404
  0.0 15.7 %copy-start.1 = (bf16[8,2,16,5120]{3,2,1,0:T(8,128)(2,1)S(1)}, bf16[8,2,16,5120]{3,2,1,0:T(8,128)(2,1)}, u32[]{:S(2)}) copy-start(bf16[8,2,16,5120]{3,2,1,0:T(8,128)(2,1)} %down_ref.3) | copy-start | bytes 7864324
  0.0 15.6 %collective-permute-start.1 = (bf16[64,1280]{1,0:T(8,128)(2,1)}, bf16[64,1280]{1,0:T(8,128)(2,1)S(1)}, u32[]{:S(2)}, u32[]{:S(2)}) collective-permute-start(bf16[64,1280]{1,0:T(8,128)(2,1)} %refs_0_.1), channel_id=1, source_target_pairs={{8,0},{12,4},{0,8},{4,12},{9,1},{13,5},{1,9},{5,13},{10,2},{14,6},... | collective-permute-start | bytes 491528 | tf_op jit(solution)/shard_map/ppermute | solution.py:28
  3.0 12.7 %collective-permute-start = (bf16[64,1280]{1,0:T(8,128)(2,1)}, bf16[64,1280]{1,0:T(8,128)(2,1)S(1)}, u32[]{:S(2)}, u32[]{:S(2)}) collective-permute-start(bf16[64,1280]{1,0:T(8,128)(2,1)} %refs_0_.1), channel_id=1, source_target_pairs={{0,4},{4,0},{8,12},{12,8},{1,5},{5,1},{9,13},{13,9},{2,6},{6,2},{1... | collective-permute-start | bytes 491528 | tf_op jit(solution)/shard_map/ppermute | solution.py:23
  3.0 12.7 %collective-permute-start.2 = (bf16[64,1280]{1,0:T(8,128)(2,1)}, bf16[64,1280]{1,0:T(8,128)(2,1)S(1)}, u32[]{:S(2)}, u32[]{:S(2)}) collective-permute-start(bf16[64,1280]{1,0:T(8,128)(2,1)} %refs_0_.1), channel_id=1, source_target_pairs={{12,0},{8,4},{4,8},{0,12},{13,1},{9,5},{5,9},{1,13},{14,2},{10,6},... | collective-permute-start | bytes 491528 | tf_op jit(solution)/shard_map/ppermute | solution.py:28
  4.1 11.6 %copy-start.3 = (s32[64]{0:T(128)S(1)}, s32[64]{0:T(128)}, u32[]{:S(2)}) copy-start(s32[64]{0:T(128)} %param.14) | copy-start | bytes 772
  4.1 11.6 %copy-start.4 = (s32[32]{0:T(128)S(1)}, s32[32]{0:T(128)}, u32[]{:S(2)}) copy-start(s32[32]{0:T(128)} %param.15) | copy-start | bytes 388
  17.9 1.7 %collective-permute-start.9 = (bf16[2,32,2560]{2,1,0:T(8,128)(2,1)S(1)}, bf16[2,32,2560]{2,1,0:T(8,128)(2,1)S(1)}, u32[]{:S(2)}, u32[]{:S(2)}) collective-permute-start(bf16[2,32,2560]{2,1,0:T(8,128)(2,1)S(1)} %get-tuple-element.31), channel_id=1, source_target_pairs={{0,4},{4,0},{8,12},{12,8},{1,5},{5,1},{9,13},{13,9},{2,6},{6,2},{1... | collective-permute-start | bytes 983048 | tf_op jit(solution)/shard_map/ppermute | solution.py:23
  18.2 3.4 %collective-permute-start.4 = (bf16[2,32,2560]{2,1,0:T(8,128)(2,1)S(1)}, bf16[2,32,2560]{2,1,0:T(8,128)(2,1)S(1)}, u32[]{:S(2)}, u32[]{:S(2)}) collective-permute-start(bf16[2,32,2560]{2,1,0:T(8,128)(2,1)S(1)} %get-tuple-element.25), channel_id=1, source_target_pairs={{0,4},{4,0},{8,12},{12,8},{1,5},{5,1},{9,13},{13,9},{2,6},{6,2},{1... | collective-permute-start | bytes 983048 | tf_op jit(solution)/shard_map/ppermute | solution.py:23
  18.4 3.7 %collective-permute-start.3 = (bf16[2,32,1280]{2,1,0:T(8,128)(2,1)S(1)}, bf16[2,32,1280]{2,1,0:T(8,128)(2,1)S(1)}, u32[]{:S(2)}, u32[]{:S(2)}) collective-permute-start(bf16[2,32,1280]{2,1,0:T(8,128)(2,1)S(1)} %get-tuple-element.22), channel_id=1, source_target_pairs={{0,4},{4,0},{8,12},{12,8},{1,5},{5,1},{9,13},{13,9},{2,6},{6,2},{1... | collective-permute-start | bytes 491528 | tf_op jit(solution)/shard_map/ppermute | solution.py:23
  19.6 8.1 %collective-permute-start.10 = (bf16[2,16,2560]{2,1,0:T(8,128)(2,1)S(1)}, bf16[2,16,2560]{2,1,0:T(8,128)(2,1)S(1)}, u32[]{:S(2)}, u32[]{:S(2)}) collective-permute-start(bf16[2,16,2560]{2,1,0:T(8,128)(2,1)S(1)} %get-tuple-element.33), channel_id=1, source_target_pairs={{8,0},{12,4},{0,8},{4,12},{9,1},{13,5},{1,9},{5,13},{10,2},{14,6},... | collective-permute-start | bytes 491528 | tf_op jit(solution)/shard_map/ppermute | solution.py:28
  21.7 8.5 %collective-permute-start.5 = (bf16[2,16,2560]{2,1,0:T(8,128)(2,1)S(1)}, bf16[2,16,2560]{2,1,0:T(8,128)(2,1)S(1)}, u32[]{:S(2)}, u32[]{:S(2)}) collective-permute-start(bf16[2,16,2560]{2,1,0:T(8,128)(2,1)S(1)} %get-tuple-element.26), channel_id=1, source_target_pairs={{8,0},{12,4},{0,8},{4,12},{9,1},{13,5},{1,9},{5,13},{10,2},{14,6},... | collective-permute-start | bytes 491528 | tf_op jit(solution)/shard_map/ppermute | solution.py:28
  22.2 10.2 %collective-permute-start.14 = (bf16[2,16,1280]{2,1,0:T(8,128)(2,1)S(1)}, bf16[2,16,1280]{2,1,0:T(8,128)(2,1)S(1)}, u32[]{:S(2)}, u32[]{:S(2)}) collective-permute-start(bf16[2,16,1280]{2,1,0:T(8,128)(2,1)S(1)} %get-tuple-element.34), channel_id=1, source_target_pairs={{8,0},{12,4},{0,8},{4,12},{9,1},{13,5},{1,9},{5,13},{10,2},{14,6},... | collective-permute-start | bytes 245768 | tf_op jit(solution)/shard_map/ppermute | solution.py:28
  27.8 6.8 %collective-permute-start.11 = (bf16[16,2560]{1,0:T(8,128)(2,1)S(1)}, bf16[16,2560]{1,0:T(8,128)(2,1)S(1)}, u32[]{:S(2)}, u32[]{:S(2)}) collective-permute-start(bf16[16,2560]{1,0:T(8,128)(2,1)S(1)} %activate.4.refs_4_), channel_id=1, source_target_pairs={{8,0},{12,4},{0,8},{4,12},{9,1},{13,5},{1,9},{5,13},{10,2},{14,6},... | collective-permute-start | bytes 245768 | tf_op jit(solution)/shard_map/ppermute | solution.py:28
  30.3 4.6 %collective-permute-start.6 = (bf16[16,2560]{1,0:T(8,128)(2,1)S(1)}, bf16[16,2560]{1,0:T(8,128)(2,1)S(1)}, u32[]{:S(2)}, u32[]{:S(2)}) collective-permute-start(bf16[16,2560]{1,0:T(8,128)(2,1)S(1)} %activate.3.refs_0_), channel_id=1, source_target_pairs={{8,0},{12,4},{0,8},{4,12},{9,1},{13,5},{1,9},{5,13},{10,2},{14,6},... | collective-permute-start | bytes 245768 | tf_op jit(solution)/shard_map/ppermute | solution.py:28
  32.4 1.9 %collective-permute-start.16 = (bf16[16,1280]{1,0:T(8,128)(2,1)S(1)}, bf16[16,1280]{1,0:T(8,128)(2,1)S(1)}, u32[]{:S(2)}, u32[]{:S(2)}) collective-permute-start(bf16[16,1280]{1,0:T(8,128)(2,1)S(1)} %activate.5.refs_8_), channel_id=1, source_target_pairs={{0,4},{4,0},{8,12},{12,8},{1,5},{5,1},{9,13},{13,9},{2,6},{6,2},{1... | collective-permute-start | bytes 122888 | tf_op jit(solution)/shard_map/ppermute | solution.py:23
  32.4 4.1 %collective-permute-start.15 = (bf16[16,1280]{1,0:T(8,128)(2,1)S(1)}, bf16[16,1280]{1,0:T(8,128)(2,1)S(1)}, u32[]{:S(2)}, u32[]{:S(2)}) collective-permute-start(bf16[16,1280]{1,0:T(8,128)(2,1)S(1)} %activate.5.refs_8_), channel_id=1, source_target_pairs={{8,0},{12,4},{0,8},{4,12},{9,1},{13,5},{1,9},{5,13},{10,2},{14,6},... | collective-permute-start | bytes 122888 | tf_op jit(solution)/shard_map/ppermute | solution.py:28
  34.1 3.6 %collective-permute-start.12 = (bf16[16,2560]{1,0:T(8,128)(2,1)S(1)}, bf16[16,2560]{1,0:T(8,128)(2,1)S(1)}, u32[]{:S(2)}, u32[]{:S(2)}) collective-permute-start(bf16[16,2560]{1,0:T(8,128)(2,1)S(1)} %activate.4.refs_4_), channel_id=1, source_target_pairs={{0,4},{4,0},{8,12},{12,8},{1,5},{5,1},{9,13},{13,9},{2,6},{6,2},{1... | collective-permute-start | bytes 245768 | tf_op jit(solution)/shard_map/ppermute | solution.py:23
  34.3 3.4 %collective-permute-start.7 = (bf16[16,2560]{1,0:T(8,128)(2,1)S(1)}, bf16[16,2560]{1,0:T(8,128)(2,1)S(1)}, u32[]{:S(2)}, u32[]{:S(2)}) collective-permute-start(bf16[16,2560]{1,0:T(8,128)(2,1)S(1)} %activate.3.refs_0_), channel_id=1, source_target_pairs={{0,4},{4,0},{8,12},{12,8},{1,5},{5,1},{9,13},{13,9},{2,6},{6,2},{1... | collective-permute-start | bytes 245768 | tf_op jit(solution)/shard_map/ppermute | solution.py:23
  34.6 3.1 %collective-permute-start.13 = (bf16[16,2560]{1,0:T(8,128)(2,1)S(1)}, bf16[16,2560]{1,0:T(8,128)(2,1)S(1)}, u32[]{:S(2)}, u32[]{:S(2)}) collective-permute-start(bf16[16,2560]{1,0:T(8,128)(2,1)S(1)} %collective-permute-done.11.refs_5_), channel_id=1, source_target_pairs={{0,4},{4,0},{8,12},{12,8},{1,5},{5,1},{9,13},{13,9},{2,6},{6,2},{1... | collective-permute-start | bytes 245768 | tf_op jit(solution)/shard_map/ppermute | solution.py:23
  34.9 2.8 %collective-permute-start.8 = (bf16[16,2560]{1,0:T(8,128)(2,1)S(1)}, bf16[16,2560]{1,0:T(8,128)(2,1)S(1)}, u32[]{:S(2)}, u32[]{:S(2)}) collective-permute-start(bf16[16,2560]{1,0:T(8,128)(2,1)S(1)} %collective-permute-done.6.refs_1_), channel_id=1, source_target_pairs={{0,4},{4,0},{8,12},{12,8},{1,5},{5,1},{9,13},{13,9},{2,6},{6,2},{1... | collective-permute-start | bytes 245768 | tf_op jit(solution)/shard_map/ppermute | solution.py:23
  36.5 1.2 %collective-permute-start.17 = (bf16[16,1280]{1,0:T(8,128)(2,1)S(1)}, bf16[16,1280]{1,0:T(8,128)(2,1)S(1)}, u32[]{:S(2)}, u32[]{:S(2)}) collective-permute-start(bf16[16,1280]{1,0:T(8,128)(2,1)S(1)} %collective-permute-done.15.refs_9_), channel_id=1, source_target_pairs={{0,4},{4,0},{8,12},{12,8},{1,5},{5,1},{9,13},{13,9},{2,6},{6,2},{1... | collective-permute-start | bytes 122888 | tf_op jit(solution)/shard_map/ppermute | solution.py:23
  42.3 6.3 %collective-permute-start.18 = (bf16[64,1280]{1,0:T(8,128)(2,1)S(1)}, bf16[64,1280]{1,0:T(8,128)(2,1)S(1)}, u32[]{:S(2)}, u32[]{:S(2)}) collective-permute-start(bf16[64,1280]{1,0:T(8,128)(2,1)S(1)} %project.1), channel_id=1, source_target_pairs={{0,1},{1,0},{2,3},{3,2},{4,5},{5,4},{6,7},{7,6},{8,9},{9,8},{10,11... | collective-permute-start | bytes 491528 | tf_op jit(solution)/shard_map/ppermute | solution.py:337
  48.6 7.6 %collective-permute-start.19 = (bf16[64,1280]{1,0:T(8,128)(2,1)S(1)}, bf16[64,1280]{1,0:T(8,128)(2,1)S(1)}, u32[]{:S(2)}, u32[]{:S(2)}) collective-permute-start(bf16[64,1280]{1,0:T(8,128)(2,1)S(1)} %add_convert_fusion.1), channel_id=1, source_target_pairs={{0,3},{1,2},{2,1},{3,0},{4,7},{5,6},{6,5},{7,4},{8,11},{9,10},{10,... | collective-permute-start | bytes 491528 | tf_op jit(solution)/shard_map/ppermute | solution.py:337
  (1 other events, 0.9 us)

commit v4 on v3

--- a/solution.py
+++ b/solution.py
@@ -12,7 +12,8 @@
 bf16 = jnp.bfloat16
 MIB = 1 << 20
 CHUNKS = (2560, 2560, 1280)
-PIECE = 256
+PIECE = 512
+TILE = 256
 
 
 def dot(a, b):
@@ -149,11 +150,10 @@
     far = pl.BlockSpec(memory_space=pltpu.HBM)
     return pl.pallas_call(
         functools.partial(stream_kernel, block, chips, start, tile),
-        out_shape=jax.ShapeDtypeStruct((2, rows, width), f32),
+        out_shape=[jax.ShapeDtypeStruct((2, rows, width), f32), jax.ShapeDtypeStruct(x.shape, bf16)],
         in_specs=[far] * 3,
-        out_specs=pl.BlockSpec(memory_space=pltpu.VMEM),
+        out_specs=[pl.BlockSpec(memory_space=pltpu.VMEM)] * 2,
         scratch_shapes=[
-            pltpu.VMEM((rows, depth), bf16),
             pltpu.VMEM((rows, depth), bf16),
             pltpu.VMEM((slots, depth, tile), bf16),
             pltpu.SemaphoreType.DMA((slots + 1,)),
@@ -235,7 +235,7 @@
 
 
 def project_kernel(count, near_ref, down_ref, *refs):
-    blocks, (total_ref, hidden, held, arrived) = refs[:-4], refs[-4:]
+    blocks, (total_ref, hidden, early, held, arrived) = refs[:-5], refs[-5:]
     pieces, depth, columns = held.shape
     near = near_ref.shape[0]
 
@@ -256,11 +256,14 @@
             at = (chip * 2 + (me + nth // chips) % 2) * block
             hidden[pl.ds(pl.multiple_of(at, 16), block), start : start + width] = ref[...]
         start += width
-    total = dot(hidden[:, :near], near_ref[...])
+    cuts = [slice(at, min(at + TILE, columns)) for at in range(0, columns, TILE)]
+    for cut in cuts:
+        early[:, cut] = dot(hidden[:, :near], near_ref[:, cut])
     for i in range(pieces):
         bring(i).wait()
-        total += dot(hidden[:, near + i * depth : near + (i + 1) * depth], held[i])
-    total_ref[...] = total.astype(bf16)
+    for cut in cuts:
+        late = dot(hidden[:, near:], held[:, :, cut].reshape(pieces * depth, -1))
+        total_ref[:, cut] = (early[:, cut] + late).astype(bf16)
 
 
 def project(chunks, near, down):
@@ -269,7 +272,8 @@
     vmem = pl.BlockSpec(memory_space=pltpu.VMEM)
     far = pl.BlockSpec(memory_space=pltpu.HBM)
     blocks = [value for chunk in chunks for value in chunk]
-    pieces = (down.shape[0] - near.shape[0]) // PIECE
+    piece = PIECE if (down.shape[0] - near.shape[0]) % PIECE == 0 else PIECE // 2
+    pieces = (down.shape[0] - near.shape[0]) // piece
     return pl.pallas_call(
         functools.partial(project_kernel, count),
         out_shape=jax.ShapeDtypeStruct((rows, down.shape[1]), bf16),
@@ -277,7 +281,8 @@
         out_specs=vmem,
         scratch_shapes=[
             pltpu.VMEM((rows, down.shape[0]), bf16),
-            pltpu.VMEM((pieces, PIECE, down.shape[1]), bf16),
+            pltpu.VMEM((rows, down.shape[1]), f32),
+            pltpu.VMEM((pieces, piece, down.shape[1]), bf16),
             pltpu.SemaphoreType.DMA((pieces,)),
         ],
         compiler_params=pltpu.CompilerParams(vmem_limit_bytes=40 * MIB),
@@ -309,7 +314,7 @@
         return [at + flip * (1 - 2 * (at % 2)) for at, flip in near + far]
 
     widths = CHUNKS if sum(CHUNKS) == units else (units,)
-    base = stream(tokens, gate_matrix, up_matrix, block, chips, 0, units)
+    base, pieces[0] = stream(tokens, gate_matrix, up_matrix, block, chips, 0, units)
     expand = adapter_up.reshape(-1, units)
     spread, *parts = shrink_rows(
         pieces, sources, block, adapter_ids, adapter_slot, adapter_down, expand, base, widths[0]

time: 57.2 us -> 57 us (level)
  no operation moved by 1% of the time
where the time goes in v4:
time: 57 us; the launch traced here: 56.8 us
  Pallas kernels  22.2 us (39%)
  starting transfers between devices  19.2 us (34%)
  waiting for transfers between devices  13.5 us (24%)
  local copies, waits for them, and re-layouts  0.99 us (2%)
  other arithmetic  0.75 us (1%)
    ppermute x8, starting transfers between devices, from_chip(): return lax.ppermute(value, 'replica', pairs)  11.6 us
    pallas_call x1, Pallas kernels, stream(): pl.pallas_call(functools.partial(stream_kernel, block, chips, start, tile...  11.5 us
    ppermute x2, waiting for transfers between devices, shards(): lax.ppermute(total, 'tensor', pairs).astype(f32)  8.41 us
    ppermute x2, starting transfers between devices, shards(): lax.ppermute(total, 'tensor', pairs).astype(f32)  5.48 us
    pallas_call x1, Pallas kernels, project(): pl.pallas_call(functools.partial(project_kernel, count), out_shape=jax.Sh...  4.37 us
    pallas_call x1, Pallas kernels, fetch(): pl.pallas_call(fetch_kernel, out_shape=jax.ShapeDtypeStruct((rows, down.s...  3.8 us
    ppermute x8, waiting for transfers between devices, from_chip(): return lax.ppermute(value, 'replica', pairs)  2.85 us
    ppermute x10, waiting for transfers between devices, core_swap(): return lax.ppermute(value, 'replica', [(i, i ^ 1) for i in range(replicas)])  2.28 us
  transfers between devices with their start and end apart: 20, of which 7 were waited for; matrix products, arithmetic and copies ran while one was open for 0% of the time, Pallas kernels for 28%

profile of v4, /device:TPU:0, one launch (start us, length us, event | category | flops | bytes accessed | tf_op | source)
XLA Modules:
  0.0 56.8 jit_solution(13875560931972985274)
XLA Ops:
  0.0 0.5 collective-permute-start
  0.5 2.6 %collective-permute-start.2 = (bf16[64,1280]{1,0:T(8,128)(2,1)}, bf16[64,1280]{1,0:T(8,128)(2,1)S(1)}, u32[]{:S(2)}, u32[]{:S(2)}) collective-permute-start(bf16[64,1280]{1,0:T(8,128)(2,1)} %x_ref.1), channel_id=1, source_target_pairs={{12,0},{8,4},{4,8},{0,12},{13,1},{9,5},{5,9},{1,13},{14,2},{10,6},... | collective-permute-start | bytes 491528 | tf_op jit(solution)/shard_map/ppermute | solution.py:29
  3.1 1.0 %copy-done.2 = bf16[64,1280]{1,0:T(8,128)(2,1)S(1)} copy-done((bf16[64,1280]{1,0:T(8,128)(2,1)S(1)}, bf16[64,1280]{1,0:T(8,128)(2,1)}, u32[]{:S(2)}) %copy-start.2) | copy-done | bytes 163864
  4.1 11.5 %stream.1 = (f32[2,64,6400]{2,1,0:T(8,128)S(1)}, bf16[64,1280]{1,0:T(8,128)(2,1)S(1)}) custom-call(bf16[64,1280]{1,0:T(8,128)(2,1)S(1)} %copy-done.2, bf16[1280,6400]{1,0:T(8,128)(2,1)} %gate_ref.1, bf16[1280,6400]{1,0:T(8,128)(2,1)} %up_ref.1), custom_call_target="tpu_custom_call" | custom-call | flops 2097152000 | bytes 32768000 | tf_op jit(solution)/shard_map/stream/pallas_call | solution.py:151
  15.7 1.7 %shrink.1 = (bf16[128,256]{1,0:T(8,128)(2,1)S(1)}, f32[2,32,2560]{2,1,0:T(8,128)S(1)}, bf16[2,32,2560]{2,1,0:T(8,128)(2,1)S(1)}) custom-call(s32[1,64]{1,0:T(1,128)S(1)} %bitcast.5, s32[1,32]{1,0:T(1,128)S(1)} %bitcast.6, bf16[8,2,16,5120]{3,2,1,0:T(8,128)(2,1)S(1)} %copy-done.1, bf16[256,6400]{1,0:T(8,128)(2,1)S(1)} %bitcast.3, ...), custom_call_target="tpu_custom_call" | custom-call | flops 167772160 | bytes 2621440 | tf_op jit(solution)/shard_map/shrink/pallas_call | solution.py:87
  17.4 0.4 widen.1
  18.0 0.4 collective-permute-start.4
  18.5 1.0 %collective-permute-done.9.got_ref = bf16[2,32,2560]{2,1,0:T(8,128)(2,1)S(1)} collective-permute-done((bf16[2,32,2560]{2,1,0:T(8,128)(2,1)S(1)}, bf16[2,32,2560]{2,1,0:T(8,128)(2,1)S(1)}, u32[]{:S(2)}, u32[]{:S(2)}) %collective-permute-start.9) | collective-permute-done | bytes 327712 | tf_op jit(solution)/shard_map/ppermute | solution.py:24
  19.6 2.0 %collective-permute-start.10 = (bf16[2,16,2560]{2,1,0:T(8,128)(2,1)S(1)}, bf16[2,16,2560]{2,1,0:T(8,128)(2,1)S(1)}, u32[]{:S(2)}, u32[]{:S(2)}) collective-permute-start(bf16[2,16,2560]{2,1,0:T(8,128)(2,1)S(1)} %get-tuple-element.37), channel_id=1, source_target_pairs={{8,0},{12,4},{0,8},{4,12},{9,1},{13,5},{1,9},{5,13},{10,2},{14,6},... | collective-permute-start | bytes 491528 | tf_op jit(solution)/shard_map/ppermute | solution.py:29
  21.7 0.4 collective-permute-start.5
  22.2 1.8 %collective-permute-start.14 = (bf16[2,16,1280]{2,1,0:T(8,128)(2,1)S(1)}, bf16[2,16,1280]{2,1,0:T(8,128)(2,1)S(1)}, u32[]{:S(2)}, u32[]{:S(2)}) collective-permute-start(bf16[2,16,1280]{2,1,0:T(8,128)(2,1)S(1)} %get-tuple-element.38), channel_id=1, source_target_pairs={{8,0},{12,4},{0,8},{4,12},{9,1},{13,5},{1,9},{5,13},{10,2},{14,6},... | collective-permute-start | bytes 245768 | tf_op jit(solution)/shard_map/ppermute | solution.py:29
  23.9 3.8 %fetch.1.near_ref = bf16[3840,1280]{1,0:T(8,128)(2,1)S(1)} custom-call(bf16[6400,1280]{1,0:T(8,128)(2,1)} %down_ref.5, f32[2,16,1280]{2,1,0:T(8,128)S(1)} %get-tuple-element.27.after_ref.own_ref), custom_call_target="tpu_custom_call" | custom-call | flops 1 | bytes 1 | tf_op jit(solution)/shard_map/fetch/pallas_call | solution.py:225
  27.8 1.0 %collective-permute-start.11 = (bf16[16,2560]{1,0:T(8,128)(2,1)S(1)}, bf16[16,2560]{1,0:T(8,128)(2,1)S(1)}, u32[]{:S(2)}, u32[]{:S(2)}) collective-permute-start(bf16[16,2560]{1,0:T(8,128)(2,1)S(1)} %activate.4.refs_4_), channel_id=1, source_target_pairs={{8,0},{12,4},{0,8},{4,12},{9,1},{13,5},{1,9},{5,13},{10,2},{14,6},... | collective-permute-start | bytes 245768 | tf_op jit(solution)/shard_map/ppermute | solution.py:29
  28.8 1.4 %collective-permute-done.5.refs_0_ = bf16[2,16,2560]{2,1,0:T(8,128)(2,1)S(1)} collective-permute-done((bf16[2,16,2560]{2,1,0:T(8,128)(2,1)S(1)}, bf16[2,16,2560]{2,1,0:T(8,128)(2,1)S(1)}, u32[]{:S(2)}, u32[]{:S(2)}) %collective-permute-start.5) | collective-permute-done | bytes 163872 | tf_op jit(solution)/shard_map/ppermute | solution.py:29
  30.3 2.0 %collective-permute-start.6 = (bf16[16,2560]{1,0:T(8,128)(2,1)S(1)}, bf16[16,2560]{1,0:T(8,128)(2,1)S(1)}, u32[]{:S(2)}, u32[]{:S(2)}) collective-permute-start(bf16[16,2560]{1,0:T(8,128)(2,1)S(1)} %activate.3.refs_0_), channel_id=1, source_target_pairs={{8,0},{12,4},{0,8},{4,12},{9,1},{13,5},{1,9},{5,13},{10,2},{14,6},... | collective-permute-start | bytes 245768 | tf_op jit(solution)/shard_map/ppermute | solution.py:29
  32.4 1.7 %collective-permute-start.15 = (bf16[16,1280]{1,0:T(8,128)(2,1)S(1)}, bf16[16,1280]{1,0:T(8,128)(2,1)S(1)}, u32[]{:S(2)}, u32[]{:S(2)}) collective-permute-start(bf16[16,1280]{1,0:T(8,128)(2,1)S(1)} %activate.5.refs_8_), channel_id=1, source_target_pairs={{8,0},{12,4},{0,8},{4,12},{9,1},{13,5},{1,9},{5,13},{10,2},{14,6},... | collective-permute-start | bytes 122888 | tf_op jit(solution)/shard_map/ppermute | solution.py:29
  35.2 1.4 %collective-permute-done.15.refs_9_ = bf16[16,1280]{1,0:T(8,128)(2,1)S(1)} collective-permute-done((bf16[16,1280]{1,0:T(8,128)(2,1)S(1)}, bf16[16,1280]{1,0:T(8,128)(2,1)S(1)}, u32[]{:S(2)}, u32[]{:S(2)}) %collective-permute-start.15) | collective-permute-done | bytes 40992 | tf_op jit(solution)/shard_map/ppermute | solution.py:29
  36.5 1.2 %collective-permute-done.17.refs_11_ = bf16[16,1280]{1,0:T(8,128)(2,1)S(1)} collective-permute-done((bf16[16,1280]{1,0:T(8,128)(2,1)S(1)}, bf16[16,1280]{1,0:T(8,128)(2,1)S(1)}, u32[]{:S(2)}, u32[]{:S(2)}) %collective-permute-start.17) | collective-permute-done | bytes 40992 | tf_op jit(solution)/shard_map/ppermute | solution.py:24
  37.8 4.4 %project.1 = bf16[64,1280]{1,0:T(8,128)(2,1)S(1)} custom-call(bf16[3840,1280]{1,0:T(8,128)(2,1)S(1)} %fetch.1.near_ref, bf16[6400,1280]{1,0:T(8,128)(2,1)} %down_ref.5, bf16[16,2560]{1,0:T(8,128)(2,1)S(1)} %activate.3.refs_0_, bf16[16,2560]{1,0:T(8,128)(2,1)S(1)} %collective-permute-done.6.refs_1_, bf16[16,2560]{1,0:T(8,128)(2,1)S(1)} %collective-permute-done.7.refs_2_, ...), custom_call_target="tpu_custom_call" | custom-call | flops 1048576000 | bytes 16384000 | tf_op jit(solution)/shard_map/project/pallas_call | solution.py:277
  42.1 1.7 %collective-permute-start.18 = (bf16[64,1280]{1,0:T(8,128)(2,1)S(1)}, bf16[64,1280]{1,0:T(8,128)(2,1)S(1)}, u32[]{:S(2)}, u32[]{:S(2)}) collective-permute-start(bf16[64,1280]{1,0:T(8,128)(2,1)S(1)} %project.1), channel_id=1, source_target_pairs={{0,1},{1,0},{2,3},{3,2},{4,5},{5,4},{6,7},{7,6},{8,9},{9,8},{10,11... | collective-permute-start | bytes 491528 | tf_op jit(solution)/shard_map/ppermute | solution.py:342
  43.9 4.6 %collective-permute-done.18 = bf16[64,1280]{1,0:T(8,128)(2,1)S(1)} collective-permute-done((bf16[64,1280]{1,0:T(8,128)(2,1)S(1)}, bf16[64,1280]{1,0:T(8,128)(2,1)S(1)}, u32[]{:S(2)}, u32[]{:S(2)}) %collective-permute-start.18) | collective-permute-done | bytes 163872 | tf_op jit(solution)/shard_map/ppermute | solution.py:342
  48.5 3.8 %collective-permute-start.19 = (bf16[64,1280]{1,0:T(8,128)(2,1)S(1)}, bf16[64,1280]{1,0:T(8,128)(2,1)S(1)}, u32[]{:S(2)}, u32[]{:S(2)}) collective-permute-start(bf16[64,1280]{1,0:T(8,128)(2,1)S(1)} %add_convert_fusion.1), channel_id=1, source_target_pairs={{0,3},{1,2},{2,1},{3,0},{4,7},{5,6},{6,5},{7,4},{8,11},{9,10},{10,... | collective-permute-start | bytes 491528 | tf_op jit(solution)/shard_map/ppermute | solution.py:342
  52.3 3.8 %collective-permute-done.19 = bf16[64,1280]{1,0:T(8,128)(2,1)S(1)} collective-permute-done((bf16[64,1280]{1,0:T(8,128)(2,1)S(1)}, bf16[64,1280]{1,0:T(8,128)(2,1)S(1)}, u32[]{:S(2)}, u32[]{:S(2)}) %collective-permute-start.19) | collective-permute-done | bytes 163872 | tf_op jit(solution)/shard_map/ppermute | solution.py:342
  56.1 0.7 %add_convert_fusion = bf16[64,1280]{1,0:T(8,128)(2,1)} fusion(bf16[64,1280]{1,0:T(8,128)(2,1)S(1)} %collective-permute-done.19, bf16[64,1280]{1,0:T(8,128)(2,1)S(1)} %add_convert_fusion.1), kind=kLoop, calls=%fused_computation | loop fusion | flops 327680 | bytes 491520 | tf_op jit(solution)/shard_map/convert_element_type | solution.py:342
  (39 shorter events, 1.8 us)
Async XLA Ops:
  0.0 15.7 %copy-start = (bf16[8,2,16,6400]{3,2,1,0:T(8,128)(2,1)S(1)}, bf16[8,2,16,6400]{3,2,1,0:T(8,128)(2,1)}, u32[]{:S(2)}) copy-start(bf16[8,2,16,6400]{3,2,1,0:T(8,128)(2,1)} %param.13) | copy-start | bytes 9830404
  0.0 15.7 %copy-start.1 = (bf16[8,2,16,5120]{3,2,1,0:T(8,128)(2,1)S(1)}, bf16[8,2,16,5120]{3,2,1,0:T(8,128)(2,1)}, u32[]{:S(2)}) copy-start(bf16[8,2,16,5120]{3,2,1,0:T(8,128)(2,1)} %down_ref.3) | copy-start | bytes 7864324
  0.0 15.6 %collective-permute-start = (bf16[64,1280]{1,0:T(8,128)(2,1)}, bf16[64,1280]{1,0:T(8,128)(2,1)S(1)}, u32[]{:S(2)}, u32[]{:S(2)}) collective-permute-start(bf16[64,1280]{1,0:T(8,128)(2,1)} %x_ref.1), channel_id=1, source_target_pairs={{0,4},{4,0},{8,12},{12,8},{1,5},{5,1},{9,13},{13,9},{2,6},{6,2},{1... | collective-permute-start | bytes 491528 | tf_op jit(solution)/shard_map/ppermute | solution.py:24
  0.5 15.2 %collective-permute-start.2 = (bf16[64,1280]{1,0:T(8,128)(2,1)}, bf16[64,1280]{1,0:T(8,128)(2,1)S(1)}, u32[]{:S(2)}, u32[]{:S(2)}) collective-permute-start(bf16[64,1280]{1,0:T(8,128)(2,1)} %x_ref.1), channel_id=1, source_target_pairs={{12,0},{8,4},{4,8},{0,12},{13,1},{9,5},{5,9},{1,13},{14,2},{10,6},... | collective-permute-start | bytes 491528 | tf_op jit(solution)/shard_map/ppermute | solution.py:29
  3.1 12.6 %collective-permute-start.1 = (bf16[64,1280]{1,0:T(8,128)(2,1)}, bf16[64,1280]{1,0:T(8,128)(2,1)S(1)}, u32[]{:S(2)}, u32[]{:S(2)}) collective-permute-start(bf16[64,1280]{1,0:T(8,128)(2,1)} %x_ref.1), channel_id=1, source_target_pairs={{8,0},{12,4},{0,8},{4,12},{9,1},{13,5},{1,9},{5,13},{10,2},{14,6},... | collective-permute-start | bytes 491528 | tf_op jit(solution)/shard_map/ppermute | solution.py:29
  4.1 11.6 %copy-start.3 = (s32[64]{0:T(128)S(1)}, s32[64]{0:T(128)}, u32[]{:S(2)}) copy-start(s32[64]{0:T(128)} %param.14) | copy-start | bytes 772
  4.1 11.6 %copy-start.4 = (s32[32]{0:T(128)S(1)}, s32[32]{0:T(128)}, u32[]{:S(2)}) copy-start(s32[32]{0:T(128)} %param.15) | copy-start | bytes 388
  17.8 1.7 %collective-permute-start.9 = (bf16[2,32,2560]{2,1,0:T(8,128)(2,1)S(1)}, bf16[2,32,2560]{2,1,0:T(8,128)(2,1)S(1)}, u32[]{:S(2)}, u32[]{:S(2)}) collective-permute-start(bf16[2,32,2560]{2,1,0:T(8,128)(2,1)S(1)} %get-tuple-element.35), channel_id=1, source_target_pairs={{0,4},{4,0},{8,12},{12,8},{1,5},{5,1},{9,13},{13,9},{2,6},{6,2},{1... | collective-permute-start | bytes 983048 | tf_op jit(solution)/shard_map/ppermute | solution.py:24
  18.0 3.6 %collective-permute-start.4 = (bf16[2,32,2560]{2,1,0:T(8,128)(2,1)S(1)}, bf16[2,32,2560]{2,1,0:T(8,128)(2,1)S(1)}, u32[]{:S(2)}, u32[]{:S(2)}) collective-permute-start(bf16[2,32,2560]{2,1,0:T(8,128)(2,1)S(1)} %get-tuple-element.29), channel_id=1, source_target_pairs={{0,4},{4,0},{8,12},{12,8},{1,5},{5,1},{9,13},{13,9},{2,6},{6,2},{1... | collective-permute-start | bytes 983048 | tf_op jit(solution)/shard_map/ppermute | solution.py:24
  18.4 3.7 %collective-permute-start.3 = (bf16[2,32,1280]{2,1,0:T(8,128)(2,1)S(1)}, bf16[2,32,1280]{2,1,0:T(8,128)(2,1)S(1)}, u32[]{:S(2)}, u32[]{:S(2)}) collective-permute-start(bf16[2,32,1280]{2,1,0:T(8,128)(2,1)S(1)} %get-tuple-element.26), channel_id=1, source_target_pairs={{0,4},{4,0},{8,12},{12,8},{1,5},{5,1},{9,13},{13,9},{2,6},{6,2},{1... | collective-permute-start | bytes 491528 | tf_op jit(solution)/shard_map/ppermute | solution.py:24
  19.6 8.1 %collective-permute-start.10 = (bf16[2,16,2560]{2,1,0:T(8,128)(2,1)S(1)}, bf16[2,16,2560]{2,1,0:T(8,128)(2,1)S(1)}, u32[]{:S(2)}, u32[]{:S(2)}) collective-permute-start(bf16[2,16,2560]{2,1,0:T(8,128)(2,1)S(1)} %get-tuple-element.37), channel_id=1, source_target_pairs={{8,0},{12,4},{0,8},{4,12},{9,1},{13,5},{1,9},{5,13},{10,2},{14,6},... | collective-permute-start | bytes 491528 | tf_op jit(solution)/shard_map/ppermute | solution.py:29
  21.7 8.5 %collective-permute-start.5 = (bf16[2,16,2560]{2,1,0:T(8,128)(2,1)S(1)}, bf16[2,16,2560]{2,1,0:T(8,128)(2,1)S(1)}, u32[]{:S(2)}, u32[]{:S(2)}) collective-permute-start(bf16[2,16,2560]{2,1,0:T(8,128)(2,1)S(1)} %get-tuple-element.30), channel_id=1, source_target_pairs={{8,0},{12,4},{0,8},{4,12},{9,1},{13,5},{1,9},{5,13},{10,2},{14,6},... | collective-permute-start | bytes 491528 | tf_op jit(solution)/shard_map/ppermute | solution.py:29
  22.2 10.2 %collective-permute-start.14 = (bf16[2,16,1280]{2,1,0:T(8,128)(2,1)S(1)}, bf16[2,16,1280]{2,1,0:T(8,128)(2,1)S(1)}, u32[]{:S(2)}, u32[]{:S(2)}) collective-permute-start(bf16[2,16,1280]{2,1,0:T(8,128)(2,1)S(1)} %get-tuple-element.38), channel_id=1, source_target_pairs={{8,0},{12,4},{0,8},{4,12},{9,1},{13,5},{1,9},{5,13},{10,2},{14,6},... | collective-permute-start | bytes 245768 | tf_op jit(solution)/shard_map/ppermute | solution.py:29
  27.8 6.8 %collective-permute-start.11 = (bf16[16,2560]{1,0:T(8,128)(2,1)S(1)}, bf16[16,2560]{1,0:T(8,128)(2,1)S(1)}, u32[]{:S(2)}, u32[]{:S(2)}) collective-permute-start(bf16[16,2560]{1,0:T(8,128)(2,1)S(1)} %activate.4.refs_4_), channel_id=1, source_target_pairs={{8,0},{12,4},{0,8},{4,12},{9,1},{13,5},{1,9},{5,13},{10,2},{14,6},... | collective-permute-start | bytes 245768 | tf_op jit(solution)/shard_map/ppermute | solution.py:29
  30.3 4.6 %collective-permute-start.6 = (bf16[16,2560]{1,0:T(8,128)(2,1)S(1)}, bf16[16,2560]{1,0:T(8,128)(2,1)S(1)}, u32[]{:S(2)}, u32[]{:S(2)}) collective-permute-start(bf16[16,2560]{1,0:T(8,128)(2,1)S(1)} %activate.3.refs_0_), channel_id=1, source_target_pairs={{8,0},{12,4},{0,8},{4,12},{9,1},{13,5},{1,9},{5,13},{10,2},{14,6},... | collective-permute-start | bytes 245768 | tf_op jit(solution)/shard_map/ppermute | solution.py:29
  32.4 1.9 %collective-permute-start.16 = (bf16[16,1280]{1,0:T(8,128)(2,1)S(1)}, bf16[16,1280]{1,0:T(8,128)(2,1)S(1)}, u32[]{:S(2)}, u32[]{:S(2)}) collective-permute-start(bf16[16,1280]{1,0:T(8,128)(2,1)S(1)} %activate.5.refs_8_), channel_id=1, source_target_pairs={{0,4},{4,0},{8,12},{12,8},{1,5},{5,1},{9,13},{13,9},{2,6},{6,2},{1... | collective-permute-start | bytes 122888 | tf_op jit(solution)/shard_map/ppermute | solution.py:24
  32.4 4.1 %collective-permute-start.15 = (bf16[16,1280]{1,0:T(8,128)(2,1)S(1)}, bf16[16,1280]{1,0:T(8,128)(2,1)S(1)}, u32[]{:S(2)}, u32[]{:S(2)}) collective-permute-start(bf16[16,1280]{1,0:T(8,128)(2,1)S(1)} %activate.5.refs_8_), channel_id=1, source_target_pairs={{8,0},{12,4},{0,8},{4,12},{9,1},{13,5},{1,9},{5,13},{10,2},{14,6},... | collective-permute-start | bytes 122888 | tf_op jit(solution)/shard_map/ppermute | solution.py:29
  34.1 3.6 %collective-permute-start.12 = (bf16[16,2560]{1,0:T(8,128)(2,1)S(1)}, bf16[16,2560]{1,0:T(8,128)(2,1)S(1)}, u32[]{:S(2)}, u32[]{:S(2)}) collective-permute-start(bf16[16,2560]{1,0:T(8,128)(2,1)S(1)} %activate.4.refs_4_), channel_id=1, source_target_pairs={{0,4},{4,0},{8,12},{12,8},{1,5},{5,1},{9,13},{13,9},{2,6},{6,2},{1... | collective-permute-start | bytes 245768 | tf_op jit(solution)/shard_map/ppermute | solution.py:24
  34.3 3.4 %collective-permute-start.7 = (bf16[16,2560]{1,0:T(8,128)(2,1)S(1)}, bf16[16,2560]{1,0:T(8,128)(2,1)S(1)}, u32[]{:S(2)}, u32[]{:S(2)}) collective-permute-start(bf16[16,2560]{1,0:T(8,128)(2,1)S(1)} %activate.3.refs_0_), channel_id=1, source_target_pairs={{0,4},{4,0},{8,12},{12,8},{1,5},{5,1},{9,13},{13,9},{2,6},{6,2},{1... | collective-permute-start | bytes 245768 | tf_op jit(solution)/shard_map/ppermute | solution.py:24
  34.6 3.1 %collective-permute-start.13 = (bf16[16,2560]{1,0:T(8,128)(2,1)S(1)}, bf16[16,2560]{1,0:T(8,128)(2,1)S(1)}, u32[]{:S(2)}, u32[]{:S(2)}) collective-permute-start(bf16[16,2560]{1,0:T(8,128)(2,1)S(1)} %collective-permute-done.11.refs_5_), channel_id=1, source_target_pairs={{0,4},{4,0},{8,12},{12,8},{1,5},{5,1},{9,13},{13,9},{2,6},{6,2},{1... | collective-permute-start | bytes 245768 | tf_op jit(solution)/shard_map/ppermute | solution.py:24
  34.9 2.8 %collective-permute-start.8 = (bf16[16,2560]{1,0:T(8,128)(2,1)S(1)}, bf16[16,2560]{1,0:T(8,128)(2,1)S(1)}, u32[]{:S(2)}, u32[]{:S(2)}) collective-permute-start(bf16[16,2560]{1,0:T(8,128)(2,1)S(1)} %collective-permute-done.6.refs_1_), channel_id=1, source_target_pairs={{0,4},{4,0},{8,12},{12,8},{1,5},{5,1},{9,13},{13,9},{2,6},{6,2},{1... | collective-permute-start | bytes 245768 | tf_op jit(solution)/shard_map/ppermute | solution.py:24
  36.5 1.2 %collective-permute-start.17 = (bf16[16,1280]{1,0:T(8,128)(2,1)S(1)}, bf16[16,1280]{1,0:T(8,128)(2,1)S(1)}, u32[]{:S(2)}, u32[]{:S(2)}) collective-permute-start(bf16[16,1280]{1,0:T(8,128)(2,1)S(1)} %collective-permute-done.15.refs_9_), channel_id=1, source_target_pairs={{0,4},{4,0},{8,12},{12,8},{1,5},{5,1},{9,13},{13,9},{2,6},{6,2},{1... | collective-permute-start | bytes 122888 | tf_op jit(solution)/shard_map/ppermute | solution.py:24
  42.1 6.3 %collective-permute-start.18 = (bf16[64,1280]{1,0:T(8,128)(2,1)S(1)}, bf16[64,1280]{1,0:T(8,128)(2,1)S(1)}, u32[]{:S(2)}, u32[]{:S(2)}) collective-permute-start(bf16[64,1280]{1,0:T(8,128)(2,1)S(1)} %project.1), channel_id=1, source_target_pairs={{0,1},{1,0},{2,3},{3,2},{4,5},{5,4},{6,7},{7,6},{8,9},{9,8},{10,11... | collective-permute-start | bytes 491528 | tf_op jit(solution)/shard_map/ppermute | solution.py:342
  48.5 7.6 %collective-permute-start.19 = (bf16[64,1280]{1,0:T(8,128)(2,1)S(1)}, bf16[64,1280]{1,0:T(8,128)(2,1)S(1)}, u32[]{:S(2)}, u32[]{:S(2)}) collective-permute-start(bf16[64,1280]{1,0:T(8,128)(2,1)S(1)} %add_convert_fusion.1), channel_id=1, source_target_pairs={{0,3},{1,2},{2,1},{3,0},{4,7},{5,6},{6,5},{7,4},{8,11},{9,10},{10,... | collective-permute-start | bytes 491528 | tf_op jit(solution)/shard_map/ppermute | solution.py:342
  (1 other events, 1.0 us)
